TPU v7x, 256 devices: a whole 4x4x8 slice. The times are simulated.
256 devices in a mesh: row: 8 (over y, z_hi), col: 8 (over z_lo, core), depth: 4 (over x).
Axes of the slice: x: 4, y: 4, z: 8 (z_hi: 2, z_lo: 4; z = z_hi * 4 + z_lo), core: 2. Of those that a mesh axis runs over, the one named last changes fastest.
Arguments:
- left_tiles: float32 [8, 8, 4, 32, 4096], P('row', 'col', 'depth'), may hold values from -2 to 2
- right_tiles: float32 [8, 8, 4, 1, 32, 4096], P('row', 'col', 'depth'), may hold values from -2 to 2
- square_tiles: float32 [8, 8, 128, 4096], P('row', 'col', 'depth'), may hold values from -4 to 4
- pairs: int32 [8, 8, 4, 8, 3, 64], P('row', 'col', 'depth'), may hold values from 0 to 127, as said below
- counts: int32 [8, 8, 4, 8], P('row', 'col', 'depth'), may hold values from 1 to 64
Outputs:
- purified: float32 [8, 8, 128, 4096], P('row', 'col', 'depth')
Inputs may be any that keep to these rules, and one draw needn't show every extreme that they name: pairs[..., 0, :] lies below 32, pairs[..., 1, :] below 32, pairs[..., 2, :] below 128; entries at or beyond the count are padding with valid slots.
All inputs are finite; a program needn't handle non-finite values.
Results may differ from a plain program's by a relative error of at most 0.0003.
Values sent between devices are 32-bit elements; how exact they have to be, the bound alone decides.
No kernel may reach another device: no remote copies, remote signals or barrier semaphores. Data moves between devices by JAX's collectives and lax.ppermute only.
A program may use at most 64 MiB of HBM per device.

v0:
```python
import functools

import jax
import jax.numpy as jnp
from jax import lax
from jax.experimental import pallas as pl
from jax.experimental.pallas import tpu as pltpu
from jax.sharding import PartitionSpec as P

AXES = ("row", "col", "depth")
F32 = jnp.float32
BF16 = jnp.bfloat16
TILES = 32
SLOTS = 128
UNROLL = 32
PARTS = ((0, 32), (32, 48), (48, 80), (80, 112), (112, 128))


def moved(x, target):
    pairs = []
    for y in range(4):
        for zh in range(2):
            for zl in range(4):
                for c in range(2):
                    for d in range(4):
                        ty, th, tl, tc, td = target(y, zh, zl, c, d)
                        source = ((y * 2 + zh) * 8 + zl * 2 + c) * 4 + d
                        dest = ((ty % 4 * 2 + th % 2) * 8 + tl % 4 * 2 + tc % 2) * 4 + td % 4
                        pairs.append((source, dest))
    return lax.ppermute(x, AXES, pairs)


def by_y(x, k):
    return moved(x, lambda y, zh, zl, c, d: (y + k, zh, zl, c, d))


def by_zl(x, k):
    return moved(x, lambda y, zh, zl, c, d: (y, zh, zl + k, c, d))


def by_depth(x, k):
    return moved(x, lambda y, zh, zl, c, d: (y, zh, zl, c, d + k))


def swap_zh(x):
    return moved(x, lambda y, zh, zl, c, d: (y, zh + 1, zl, c, d))


def swap_core(x):
    return moved(x, lambda y, zh, zl, c, d: (y, zh, zl, c + 1, d))


def split(p):
    high = p.astype(BF16).astype(F32)
    return high, p - high


def section_kernel(jobs, later, n_left, n_right, n_made, has_acc, half, *refs):
    def take(n):
        nonlocal refs
        taken, refs = refs[:n], refs[n:]
        return taken

    place, pairs, counts = take(3)
    lefts, rights, made = take(n_left), take(n_right), take(n_made)
    start = take(1) if has_acc else ()
    outs = take(len(PARTS)) if half is not None else ()
    out = take(1)[0]
    splits = take(len(later))
    a3, b3 = take(2)
    rows = take(1)[0] if rights else None
    shift, core, depth = place[0], place[1], place[2]
    lane = lax.broadcasted_iota(jnp.int32, (32, 128), 1) < 64
    height = out.shape[1]
    lane_left = lane[:height]

    def section(job):
        k, odd = job[0], job[1]
        return lax.rem(2 * k + 9 - 2 * core, 8) if odd else 2 * k

    def split_left(left, t):
        p = left[t] if half is None else left[t, height * half : height * half + height]
        h, low = split(p)
        hr = pltpu.roll(h, 64, 1)
        lr = pltpu.roll(low, 64, 1)
        a3[t, 0:height] = jnp.where(lane_left, h, hr).astype(BF16)
        a3[t, height : 2 * height] = jnp.where(lane_left, hr, h).astype(BF16)
        a3[t, 2 * height : 3 * height] = jnp.where(lane_left, low, lr).astype(BF16)
        a3[t, 3 * height : 4 * height] = jnp.where(lane_left, lr, low).astype(BF16)

    def split_right(job, target):
        k, _, _, choices = job

        def interleave(ref):
            @pl.loop(0, TILES, unroll=4)
            def _(t):
                r = ref[t]
                rr = pltpu.roll(r, 64, 1)
                rows[t, pl.ds(0, 32, stride=2)] = jnp.where(lane, r, rr)
                rows[t, pl.ds(1, 32, stride=2)] = jnp.where(lane, rr, r)

        if len(choices) == 1:
            interleave(rights[choices[0][1]])
        else:
            want = lax.rem(k + shift + 4, 4)
            for offset, index in choices:
                pl.when(want == offset)(functools.partial(interleave, rights[index]))

        @pl.loop(0, TILES, unroll=4)
        def _(t):
            h, low = split(rows[t])
            target[t, 0:64] = h.astype(BF16)
            target[t, 64:128] = low.astype(BF16)

    if not has_acc:
        out[...] = jnp.zeros_like(out)
    elif half is None:
        out[...] = start[0][...]
    else:
        out[...] = start[0][:, height * half : height * half + height]
    def split_panels(j):
        left = lefts[jobs[j][2]]

        @pl.loop(0, TILES, unroll=4)
        def _(t):
            split_left(left, t)
            if made:
                b3[t] = made[j][t]

        if not made:
            split_right(jobs[j], b3)

    def add_products(s):
        live = counts[s]

        @pl.loop(0, (live + UNROLL - 1) // UNROLL)
        def _(block):
            sums, slots = [], []
            for u in range(UNROLL):
                p = block * UNROLL + u
                c = jnp.dot(a3[pairs[s, 0, p]], b3[pairs[s, 1, p]], preferred_element_type=F32)
                c = c[0 : 2 * height] + c[2 * height : 4 * height]
                sums.append(jnp.where(lane_left, c[0:height], c[height : 2 * height]))
                g = lax.rem(pairs[s, 2, p] + (4 - depth) * 32, SLOTS)
                slots.append(jnp.where(p < live, g, SLOTS))
            for u in range(UNROLL):
                out[slots[u]] += sums[u]

    if len(jobs) == 1:
        split_panels(0)
        add_products(section(jobs[0]))
    else:

        @pl.loop(0, len(jobs))
        def _(now):
            s = jnp.int32(0)
            for j, job in enumerate(jobs):
                s = jnp.where(now == j, section(job), s)
                pl.when(now == j)(functools.partial(split_panels, j))
            add_products(s)

    for job, target in zip(later, splits):
        split_right(job, target)
    for ref, (first, last) in zip(outs, PARTS):
        ref[...] = out[first:last]


def add_sections(jobs, place, pattern, limits, lefts, rights, acc, name, later=[], half=None, made=[]):
    smem = pl.BlockSpec(memory_space=pltpu.SMEM)
    vmem = pl.BlockSpec(memory_space=pltpu.VMEM)
    operands = [*lefts, *rights, *made] + ([] if acc is None else [acc])
    height = 32 if half is None else 16
    sums = (SLOTS + 1, height, 128)
    shapes = [jax.ShapeDtypeStruct(sums, F32)]
    shapes += [jax.ShapeDtypeStruct((TILES, 128, 128), BF16) for _ in later]
    scratch = [pltpu.VMEM((TILES, 4 * height, 128), BF16), pltpu.VMEM((TILES, 128, 128), BF16)]
    if rights:
        scratch.append(pltpu.VMEM((TILES, 64, 128), F32))
    if half is not None:
        shapes = [jax.ShapeDtypeStruct((last - first, height, 128), F32) for first, last in PARTS]
        scratch = [pltpu.VMEM(sums, F32)] + scratch
    out = pl.pallas_call(
        functools.partial(
            section_kernel, jobs, later, len(lefts), len(rights), len(made), acc is not None, half
        ),
        out_shape=shapes,
        in_specs=[smem] * 3 + [vmem] * len(operands),
        out_specs=[vmem] * len(shapes),
        scratch_shapes=scratch,
        compiler_params=pltpu.CompilerParams(vmem_limit_bytes=28 << 20),
        cost_estimate=pl.CostEstimate(flops=0, bytes_accessed=0, transcendentals=0),
        name=name,
    )(place, pattern, limits, *operands)
    return out[0] if len(out) == 1 else out


def reduce_over_depth(parts):
    own, low, up, down, high = parts
    up, down = by_depth(up, 1), by_depth(down, -1)
    up, down = lax.optimization_barrier((up, down))
    up2 = by_depth(low + up[16:32], 1)
    down2 = by_depth(high + down[0:16], -1)
    up2, down2 = lax.optimization_barrier((up2, down2))
    return jnp.concatenate([own[0:16] + down[16:32] + up2, own[16:32] + up[0:16] + down2])


def on_device(left_tiles, right_tiles, square_tiles, pairs, counts):
    row, col = lax.axis_index("row"), lax.axis_index("col")
    core = col % 2
    place = jnp.stack([row % 2 - core, core, lax.axis_index("depth")]).astype(jnp.int32)
    pattern, limits = pairs[0, 0, 0], counts[0, 0, 0]

    right = right_tiles[0, 0, 0, 0].reshape(TILES, 32, 128)
    left = left_tiles[0, 0, 0].reshape(TILES, 32, 128)

    args = (place, pattern, limits)
    choices = [(i, i) for i in range(4)]
    other0 = swap_zh(right)
    same1, same3, same2 = by_y(right, -1), by_y(right, 1), by_y(right, 2)
    twin0 = swap_core(left)
    acc = add_sections([(0, False, 0, [(0, 0)])], *args, [left], [right], None, "sections_a")
    other0, acc, left = lax.optimization_barrier((other0, acc, left))
    left1 = by_zl(left, -1)
    same1, same3, same2, other0, acc = lax.optimization_barrier((same1, same3, same2, other0, acc))

    other1, other3, other2 = by_y(other0, -1), by_y(other0, 1), by_y(other0, 2)
    left2 = by_zl(left1, -1)
    twin1 = swap_core(left1)
    even3, odd3 = (3, False, 0, [(3, 1)]), (3, True, 0, choices)
    acc, made_even = add_sections(
        [(1, False, 0, [(1, 0)])], *args, [left1], [same1, same3], acc, "sections_b", [even3]
    )
    near = [(0, 0), (1, 1), (3, 2)]
    acc = add_sections([(0, True, 0, near)], *args, [twin0], [other0, other1, other3], acc, "sections_c")
    other1, other3, left2, acc = lax.optimization_barrier((other1, other3, left2, acc))

    left3 = by_zl(left2, -1)
    acc = add_sections([(2, False, 0, [(2, 0)])], *args, [left2], [same2], acc, "sections_d")
    twin2 = swap_core(left2)
    other = [other0, other1, other2, other3]
    jobs = [(k, True, k - 1, choices) for k in (1, 2)]
    acc, made_odd = add_sections(jobs, *args, [twin1, twin2], other, acc, "sections_e", [odd3])

    left3, acc = lax.optimization_barrier((left3, acc))
    twin3 = swap_core(left3)
    acc = add_sections([even3], *args, [left3], [], acc, "sections_f", made=[made_even])
    share = [
        add_sections([odd3], *args, [twin3], [], acc, f"sections_g{h}", [], h, [made_odd]) for h in range(2)
    ]
    share = [reduce_over_depth(half) for half in share]
    share = jnp.concatenate(share, axis=1)
    purified = 3.0 * square_tiles[0, 0] - 2.0 * share.reshape(TILES, 4096)
    return purified[None, None]


def solution(mesh):
    in_specs = (
        P("row", "col", "depth", None, None),
        P("row", "col", "depth", None, None, None),
        P("row", "col", "depth", None),
        P("row", "col", "depth", None, None, None),
        P("row", "col", "depth", None),
    )
    out_specs = P("row", "col", "depth", None)
    return jax.shard_map(
        on_device, mesh=mesh, in_specs=in_specs, out_specs=out_specs, check_vma=False
    )
```

profile of v0, /device:TPU:30, one launch (start us, length us, event | category | flops | bytes accessed | tf_op | source)
XLA Modules:
  0.0 108.2 jit_solution(10369552070514208758)
XLA Ops:
  0.0 1.1 %copy.7 = f32[4,8,32,128]{3,2,1,0:T(8,128)S(1)} copy(f32[4,8,32,128]{3,1,2,0:T(8,128)} %bitcast.39) | data formatting | bytes 1048576
  1.2 7.3 %collective-permute-start.3 = (f32[32,32,128]{2,1,0:T(8,128)S(1)}, f32[32,32,128]{2,1,0:T(8,128)S(1)}, u32[]{:S(2)}, u32[]{:S(2)}) collective-permute-start(f32[32,32,128]{2,1,0:T(8,128)S(1)} %bitcast.15), channel_id=1, source_target_pairs={{0,32},{1,33},{2,34},{3,35},{4,36},{5,37},{6,38},{7,39},{8,40},{9,... | collective-permute-start | bytes 1572872 | tf_op jit(solution)/shard_map/ppermute | solution.py:30
  8.4 1.2 %collective-permute-start.2 = (f32[32,32,128]{2,1,0:T(8,128)S(1)}, f32[32,32,128]{2,1,0:T(8,128)S(1)}, u32[]{:S(2)}, u32[]{:S(2)}) collective-permute-start(f32[32,32,128]{2,1,0:T(8,128)S(1)} %bitcast.16), channel_id=1, source_target_pairs={{0,128},{1,129},{2,130},{3,131},{4,132},{5,133},{6,134},{7,135},{8... | collective-permute-start | bytes 1572872 | tf_op jit(solution)/shard_map/ppermute | solution.py:30
  9.7 2.2 %collective-permute-start.1 = (f32[32,32,128]{2,1,0:T(8,128)S(1)}, f32[32,32,128]{2,1,0:T(8,128)S(1)}, u32[]{:S(2)}, u32[]{:S(2)}) collective-permute-start(f32[32,32,128]{2,1,0:T(8,128)S(1)} %bitcast.17), channel_id=1, source_target_pairs={{0,64},{1,65},{2,66},{3,67},{4,68},{5,69},{6,70},{7,71},{8,72},{9,... | collective-permute-start | bytes 1572872 | tf_op jit(solution)/shard_map/ppermute | solution.py:30
  11.9 0.7 copy.10
  12.6 0.1 pad_add_fusion.refs_0_
  12.6 1.1 %copy.8 = f32[4,8,32,128]{3,2,1,0:T(8,128)S(1)} copy(f32[4,8,32,128]{3,1,2,0:T(8,128)} %bitcast.40) | data formatting | bytes 1048576
  13.8 3.0 %sections_a.1.refs_6_ = f32[129,32,128]{2,1,0:T(8,128)S(1)} custom-call(s32[3]{0:T(128)S(1)} %pad_add_fusion.refs_0_, s32[8,3,64]{2,1,0:T(4,128)S(1)} %bitcast.23, s32[8]{0:T(128)S(1)} %bitcast.31, f32[32,32,128]{2,1,0:T(8,128)S(1)} %bitcast.20, f32[32,32,128]{2,1,0:T(8,128)S(1)} %bitcast.19), custom_call_target="tpu_custom_call" | custom-call | tf_op jit(solution)/shard_map/sections_a/pallas_call | solution.py:182
  16.8 5.8 %collective-permute-done.3.refs_4_.refs_5_ = f32[32,32,128]{2,1,0:T(8,128)S(1)} collective-permute-done((f32[32,32,128]{2,1,0:T(8,128)S(1)}, f32[32,32,128]{2,1,0:T(8,128)S(1)}, u32[]{:S(2)}, u32[]{:S(2)}) %collective-permute-start.3) | collective-permute-done | bytes 524320 | tf_op jit(solution)/shard_map/ppermute | solution.py:30
  22.6 7.0 %collective-permute-start.6 = (f32[32,32,128]{2,1,0:T(8,128)S(1)}, f32[32,32,128]{2,1,0:T(8,128)S(1)}, u32[]{:S(2)}, u32[]{:S(2)}) collective-permute-start(f32[32,32,128]{2,1,0:T(8,128)S(1)} %bitcast.21), channel_id=1, source_target_pairs={{0,24},{1,25},{2,26},{3,27},{4,28},{5,29},{6,30},{7,31},{8,0},{9,1... | collective-permute-start | bytes 1572872 | tf_op jit(solution)/shard_map/ppermute | solution.py:30
  29.6 2.5 %collective-permute-done.1.refs_5_ = f32[32,32,128]{2,1,0:T(8,128)S(1)} collective-permute-done((f32[32,32,128]{2,1,0:T(8,128)S(1)}, f32[32,32,128]{2,1,0:T(8,128)S(1)}, u32[]{:S(2)}, u32[]{:S(2)}) %collective-permute-start.1) | collective-permute-done | bytes 524320 | tf_op jit(solution)/shard_map/ppermute | solution.py:30
  32.1 2.4 %collective-permute-done.refs_4_ = f32[32,32,128]{2,1,0:T(8,128)S(1)} collective-permute-done((f32[32,32,128]{2,1,0:T(8,128)S(1)}, f32[32,32,128]{2,1,0:T(8,128)S(1)}, u32[]{:S(2)}, u32[]{:S(2)}) %collective-permute-start) | collective-permute-done | bytes 524320 | tf_op jit(solution)/shard_map/ppermute | solution.py:30
  34.6 0.6 collective-permute-start.5
  35.2 1.4 %collective-permute-start.4 = (f32[32,32,128]{2,1,0:T(8,128)S(1)}, f32[32,32,128]{2,1,0:T(8,128)S(1)}, u32[]{:S(2)}, u32[]{:S(2)}) collective-permute-start(f32[32,32,128]{2,1,0:T(8,128)S(1)} %collective-permute-done.3.refs_4_.refs_5_), channel_id=1, source_target_pairs={{0,192},{1,193},{2,194},{3,195},{4,196},{5,197},{6,198},{7,199},{8... | collective-permute-start | bytes 1572872 | tf_op jit(solution)/shard_map/ppermute | solution.py:30
  36.6 7.4 %collective-permute-done.6.refs_3_ = f32[32,32,128]{2,1,0:T(8,128)S(1)} collective-permute-done((f32[32,32,128]{2,1,0:T(8,128)S(1)}, f32[32,32,128]{2,1,0:T(8,128)S(1)}, u32[]{:S(2)}, u32[]{:S(2)}) %collective-permute-start.6) | collective-permute-done | bytes 524320 | tf_op jit(solution)/shard_map/ppermute | solution.py:30
  44.0 1.8 %collective-permute-start.7 = (f32[32,32,128]{2,1,0:T(8,128)S(1)}, f32[32,32,128]{2,1,0:T(8,128)S(1)}, u32[]{:S(2)}, u32[]{:S(2)}) collective-permute-start(f32[32,32,128]{2,1,0:T(8,128)S(1)} %collective-permute-done.6.refs_3_), channel_id=1, source_target_pairs={{0,24},{1,25},{2,26},{3,27},{4,28},{5,29},{6,30},{7,31},{8,0},{9,1... | collective-permute-start | bytes 1572872 | tf_op jit(solution)/shard_map/ppermute | solution.py:30
  45.8 1.2 %collective-permute-start.12 = (f32[32,32,128]{2,1,0:T(8,128)S(1)}, f32[32,32,128]{2,1,0:T(8,128)S(1)}, u32[]{:S(2)}, u32[]{:S(2)}) collective-permute-start(f32[32,32,128]{2,1,0:T(8,128)S(1)} %collective-permute-done.3.refs_4_.refs_5_), channel_id=1, source_target_pairs={{0,128},{1,129},{2,130},{3,131},{4,132},{5,133},{6,134},{7,135},{8... | collective-permute-start | bytes 1572872 | tf_op jit(solution)/shard_map/ppermute | solution.py:30
  47.0 3.8 %sections_b.1 = (f32[129,32,128]{2,1,0:T(8,128)S(1)}, bf16[32,128,128]{2,1,0:T(8,128)(2,1)S(1)}) custom-call(s32[3]{0:T(128)S(1)} %pad_add_fusion.refs_0_, s32[8,3,64]{2,1,0:T(4,128)S(1)} %bitcast.24, s32[8]{0:T(128)S(1)} %bitcast.32, f32[32,32,128]{2,1,0:T(8,128)S(1)} %collective-permute-done.6.refs_3_, f32[32,32,128]{2,1,0:T(8,128)S(1)} %collective-permute-done.refs_4_, ...), custom_call_target="tpu_custom_call" | custom-call | tf_op jit(solution)/shard_map/sections_b/pallas_call | solution.py:182
  50.8 0.1 collective-permute-start.10
  50.9 9.9 %collective-permute-done.4.refs_5_.refs_6_ = f32[32,32,128]{2,1,0:T(8,128)S(1)} collective-permute-done((f32[32,32,128]{2,1,0:T(8,128)S(1)}, f32[32,32,128]{2,1,0:T(8,128)S(1)}, u32[]{:S(2)}, u32[]{:S(2)}) %collective-permute-start.4) | collective-permute-done | bytes 524320 | tf_op jit(solution)/shard_map/ppermute | solution.py:30
  60.8 3.0 %sections_c.1.refs_5_ = f32[129,32,128]{2,1,0:T(8,128)S(1)} custom-call(s32[3]{0:T(128)S(1)} %pad_add_fusion.refs_0_, s32[8,3,64]{2,1,0:T(4,128)S(1)} %bitcast.25, s32[8]{0:T(128)S(1)} %bitcast.33, f32[32,32,128]{2,1,0:T(8,128)S(1)} %collective-permute-done.8.refs_3_, f32[32,32,128]{2,1,0:T(8,128)S(1)} %collective-permute-done.3.refs_4_.refs_5_, ...), custom_call_target="tpu_custom_call" | custom-call | tf_op jit(solution)/shard_map/sections_c/pallas_call | solution.py:182
  63.9 0.1 collective-permute-start.11
  64.0 2.0 %collective-permute-start.9 = (f32[32,32,128]{2,1,0:T(8,128)S(1)}, f32[32,32,128]{2,1,0:T(8,128)S(1)}, u32[]{:S(2)}, u32[]{:S(2)}) collective-permute-start(f32[32,32,128]{2,1,0:T(8,128)S(1)} %collective-permute-done.7.refs_3_), channel_id=1, source_target_pairs={{0,24},{1,25},{2,26},{3,27},{4,28},{5,29},{6,30},{7,31},{8,0},{9,1... | collective-permute-start | bytes 1572872 | tf_op jit(solution)/shard_map/ppermute | solution.py:30
  66.0 3.2 %sections_d.1.refs_9_ = f32[129,32,128]{2,1,0:T(8,128)S(1)} custom-call(s32[3]{0:T(128)S(1)} %pad_add_fusion.refs_0_, s32[8,3,64]{2,1,0:T(4,128)S(1)} %bitcast.26, s32[8]{0:T(128)S(1)} %bitcast.34, f32[32,32,128]{2,1,0:T(8,128)S(1)} %collective-permute-done.7.refs_3_, f32[32,32,128]{2,1,0:T(8,128)S(1)} %collective-permute-done.2.refs_4_, ...), custom_call_target="tpu_custom_call" | custom-call | tf_op jit(solution)/shard_map/sections_d/pallas_call | solution.py:182
  69.2 5.9 %sections_e.1 = (f32[129,32,128]{2,1,0:T(8,128)S(1)}, bf16[32,128,128]{2,1,0:T(8,128)(2,1)S(1)}) custom-call(s32[3]{0:T(128)S(1)} %pad_add_fusion.refs_0_, s32[8,3,64]{2,1,0:T(4,128)S(1)} %bitcast.27, s32[8]{0:T(128)S(1)} %bitcast.35, f32[32,32,128]{2,1,0:T(8,128)S(1)} %collective-permute-done.10.refs_3_, ...), custom_call_target="tpu_custom_call" | custom-call | tf_op jit(solution)/shard_map/sections_e/pallas_call | solution.py:182
  75.1 3.2 %collective-permute-done.9.refs_3_ = f32[32,32,128]{2,1,0:T(8,128)S(1)} collective-permute-done((f32[32,32,128]{2,1,0:T(8,128)S(1)}, f32[32,32,128]{2,1,0:T(8,128)S(1)}, u32[]{:S(2)}, u32[]{:S(2)}) %collective-permute-start.9) | collective-permute-done | bytes 524320 | tf_op jit(solution)/shard_map/ppermute | solution.py:30
  78.3 2.2 %sections_f.1.refs_5_ = f32[129,32,128]{2,1,0:T(8,128)S(1)} custom-call(s32[3]{0:T(128)S(1)} %pad_add_fusion.refs_0_, s32[8,3,64]{2,1,0:T(4,128)S(1)} %bitcast.28, s32[8]{0:T(128)S(1)} %bitcast.36, f32[32,32,128]{2,1,0:T(8,128)S(1)} %collective-permute-done.9.refs_3_, bf16[32,128,128]{2,1,0:T(8,128)(2,1)S(1)} %get-tuple-element.57.refs_4_, ...), custom_call_target="tpu_custom_call" | custom-call | tf_op jit(solution)/shard_map/sections_f/pallas_call | solution.py:182
  80.6 2.1 %sections_g1.1 = (f32[32,16,128]{2,1,0:T(8,128)S(1)}, f32[16,16,128]{2,1,0:T(8,128)S(1)}, f32[32,16,128]{2,1,0:T(8,128)S(1)}, f32[32,16,128]{2,1,0:T(8,128)S(1)}, f32[16,16,128]{2,1,0:T(8,128)S(1)}) custom-call(s32[3]{0:T(128)S(1)} %pad_add_fusion.refs_0_, s32[8,3,64]{2,1,0:T(4,128)S(1)} %bitcast.29, s32[8]{0:T(128)S(1)} %bitcast.37, ...), custom_call_target="tpu_custom_call" | custom-call | tf_op jit(solution)/shard_map/sections_g1/pallas_call | solution.py:182
  82.7 0.6 collective-permute-start.18
  83.3 1.6 %collective-permute-start.19 = (f32[32,16,128]{2,1,0:T(8,128)S(1)}, f32[32,16,128]{2,1,0:T(8,128)S(1)}, u32[]{:S(2)}, u32[]{:S(2)}) collective-permute-start(f32[32,16,128]{2,1,0:T(8,128)S(1)} %get-tuple-element.70), channel_id=1, source_target_pairs={{0,3},{1,0},{2,1},{3,2},{4,7},{5,4},{6,5},{7,6},{8,11},{9,8},{10,9... | collective-permute-start | bytes 786440 | tf_op jit(solution)/shard_map/ppermute | solution.py:30
  84.8 2.1 %sections_g0.1 = (f32[32,16,128]{2,1,0:T(8,128)S(1)}, f32[16,16,128]{2,1,0:T(8,128)S(1)}, f32[32,16,128]{2,1,0:T(8,128)S(1)}, f32[32,16,128]{2,1,0:T(8,128)S(1)}, f32[16,16,128]{2,1,0:T(8,128)S(1)}) custom-call(s32[3]{0:T(128)S(1)} %pad_add_fusion.refs_0_, s32[8,3,64]{2,1,0:T(4,128)S(1)} %bitcast.30, s32[8]{0:T(128)S(1)} %bitcast.38, ...), custom_call_target="tpu_custom_call" | custom-call | tf_op jit(solution)/shard_map/sections_g0/pallas_call | solution.py:182
  87.0 1.8 %collective-permute-start.14 = (f32[32,16,128]{2,1,0:T(8,128)S(1)}, f32[32,16,128]{2,1,0:T(8,128)S(1)}, u32[]{:S(2)}, u32[]{:S(2)}) collective-permute-start(f32[32,16,128]{2,1,0:T(8,128)S(1)} %get-tuple-element.60), channel_id=1, source_target_pairs={{0,1},{1,2},{2,3},{3,0},{4,5},{5,6},{6,7},{7,4},{8,9},{9,10},{10,1... | collective-permute-start | bytes 786440 | tf_op jit(solution)/shard_map/ppermute | solution.py:30
  88.7 0.3 collective-permute-start.15
  89.1 2.6 %collective-permute-done.18 = f32[32,16,128]{2,1,0:T(8,128)S(1)} collective-permute-done((f32[32,16,128]{2,1,0:T(8,128)S(1)}, f32[32,16,128]{2,1,0:T(8,128)S(1)}, u32[]{:S(2)}, u32[]{:S(2)}) %collective-permute-start.18) | collective-permute-done | bytes 262176 | tf_op jit(solution)/shard_map/ppermute | solution.py:30
  91.6 2.0 %collective-permute-done.19 = f32[32,16,128]{2,1,0:T(8,128)S(1)} collective-permute-done((f32[32,16,128]{2,1,0:T(8,128)S(1)}, f32[32,16,128]{2,1,0:T(8,128)S(1)}, u32[]{:S(2)}, u32[]{:S(2)}) %collective-permute-start.19) | collective-permute-done | bytes 262176 | tf_op jit(solution)/shard_map/ppermute | solution.py:30
  93.6 1.8 %collective-permute-start.20 = (f32[16,16,128]{2,1,0:T(8,128)S(1)}, f32[16,16,128]{2,1,0:T(8,128)S(1)}, u32[]{:S(2)}, u32[]{:S(2)}) collective-permute-start(f32[16,16,128]{2,1,0:T(8,128)S(1)} %slice_add_fusion.1), channel_id=1, source_target_pairs={{0,1},{1,2},{2,3},{3,0},{4,5},{5,6},{6,7},{7,4},{8,9},{9,10},{10,1... | collective-permute-start | bytes 393224 | tf_op jit(solution)/shard_map/ppermute | solution.py:30
  95.4 0.4 collective-permute-start.21
  95.8 1.4 %collective-permute-done.14 = f32[32,16,128]{2,1,0:T(8,128)S(1)} collective-permute-done((f32[32,16,128]{2,1,0:T(8,128)S(1)}, f32[32,16,128]{2,1,0:T(8,128)S(1)}, u32[]{:S(2)}, u32[]{:S(2)}) %collective-permute-start.14) | collective-permute-done | bytes 262176 | tf_op jit(solution)/shard_map/ppermute | solution.py:30
  97.2 2.0 %collective-permute-done.15 = f32[32,16,128]{2,1,0:T(8,128)S(1)} collective-permute-done((f32[32,16,128]{2,1,0:T(8,128)S(1)}, f32[32,16,128]{2,1,0:T(8,128)S(1)}, u32[]{:S(2)}, u32[]{:S(2)}) %collective-permute-start.15) | collective-permute-done | bytes 262176 | tf_op jit(solution)/shard_map/ppermute | solution.py:30
  99.2 1.5 %collective-permute-start.16 = (f32[16,16,128]{2,1,0:T(8,128)S(1)}, f32[16,16,128]{2,1,0:T(8,128)S(1)}, u32[]{:S(2)}, u32[]{:S(2)}) collective-permute-start(f32[16,16,128]{2,1,0:T(8,128)S(1)} %slice_add_fusion.3), channel_id=1, source_target_pairs={{0,1},{1,2},{2,3},{3,0},{4,5},{5,6},{6,7},{7,4},{8,9},{9,10},{10,1... | collective-permute-start | bytes 393224 | tf_op jit(solution)/shard_map/ppermute | solution.py:30
  100.8 0.7 collective-permute-start.17
  101.5 0.6 collective-permute-done.21
  102.1 2.8 %collective-permute-done.16 = f32[16,16,128]{2,1,0:T(8,128)S(1)} collective-permute-done((f32[16,16,128]{2,1,0:T(8,128)S(1)}, f32[16,16,128]{2,1,0:T(8,128)S(1)}, u32[]{:S(2)}, u32[]{:S(2)}) %collective-permute-start.16) | collective-permute-done | bytes 131104 | tf_op jit(solution)/shard_map/ppermute | solution.py:30
  104.8 2.2 %collective-permute-done.17 = f32[16,16,128]{2,1,0:T(8,128)S(1)} collective-permute-done((f32[16,16,128]{2,1,0:T(8,128)S(1)}, f32[16,16,128]{2,1,0:T(8,128)S(1)}, u32[]{:S(2)}, u32[]{:S(2)}) %collective-permute-start.17) | collective-permute-done | bytes 131104 | tf_op jit(solution)/shard_map/ppermute | solution.py:30
  107.0 0.1 add_add_fusion.1
  107.1 0.1 maximum_multiply_fusion
  107.2 0.1 mul.27
  107.3 0.8 multiply_subtract_fusion
  (20 shorter events, 0.1 us)
Async XLA Ops:
  0.0 13.8 %copy-start = (s32[1,1,1,8]{3,2,1,0:T(1,128)S(1)}, s32[1,1,1,8]{3,2,1,0:T(1,128)}, u32[]{:S(2)}) copy-start(s32[1,1,1,8]{3,2,1,0:T(1,128)} %param.9) | copy-start | bytes 100
  1.2 21.5 %collective-permute-start.3 = (f32[32,32,128]{2,1,0:T(8,128)S(1)}, f32[32,32,128]{2,1,0:T(8,128)S(1)}, u32[]{:S(2)}, u32[]{:S(2)}) collective-permute-start(f32[32,32,128]{2,1,0:T(8,128)S(1)} %bitcast.15), channel_id=1, source_target_pairs={{0,32},{1,33},{2,34},{3,35},{4,36},{5,37},{6,38},{7,39},{8,40},{9,... | collective-permute-start | bytes 1572872 | tf_op jit(solution)/shard_map/ppermute | solution.py:30
  8.4 21.2 %collective-permute-start.2 = (f32[32,32,128]{2,1,0:T(8,128)S(1)}, f32[32,32,128]{2,1,0:T(8,128)S(1)}, u32[]{:S(2)}, u32[]{:S(2)}) collective-permute-start(f32[32,32,128]{2,1,0:T(8,128)S(1)} %bitcast.16), channel_id=1, source_target_pairs={{0,128},{1,129},{2,130},{3,131},{4,132},{5,133},{6,134},{7,135},{8... | collective-permute-start | bytes 1572872 | tf_op jit(solution)/shard_map/ppermute | solution.py:30
  9.7 22.5 %collective-permute-start.1 = (f32[32,32,128]{2,1,0:T(8,128)S(1)}, f32[32,32,128]{2,1,0:T(8,128)S(1)}, u32[]{:S(2)}, u32[]{:S(2)}) collective-permute-start(f32[32,32,128]{2,1,0:T(8,128)S(1)} %bitcast.17), channel_id=1, source_target_pairs={{0,64},{1,65},{2,66},{3,67},{4,68},{5,69},{6,70},{7,71},{8,72},{9,... | collective-permute-start | bytes 1572872 | tf_op jit(solution)/shard_map/ppermute | solution.py:30
  11.8 22.7 %collective-permute-start = (f32[32,32,128]{2,1,0:T(8,128)S(1)}, f32[32,32,128]{2,1,0:T(8,128)S(1)}, u32[]{:S(2)}, u32[]{:S(2)}) collective-permute-start(f32[32,32,128]{2,1,0:T(8,128)S(1)} %bitcast.18), channel_id=1, source_target_pairs={{0,192},{1,193},{2,194},{3,195},{4,196},{5,197},{6,198},{7,199},{8... | collective-permute-start | bytes 1572872 | tf_op jit(solution)/shard_map/ppermute | solution.py:30
  22.6 21.4 %collective-permute-start.6 = (f32[32,32,128]{2,1,0:T(8,128)S(1)}, f32[32,32,128]{2,1,0:T(8,128)S(1)}, u32[]{:S(2)}, u32[]{:S(2)}) collective-permute-start(f32[32,32,128]{2,1,0:T(8,128)S(1)} %bitcast.21), channel_id=1, source_target_pairs={{0,24},{1,25},{2,26},{3,27},{4,28},{5,29},{6,30},{7,31},{8,0},{9,1... | collective-permute-start | bytes 1572872 | tf_op jit(solution)/shard_map/ppermute | solution.py:30
  29.6 21.2 %collective-permute-start.8 = (f32[32,32,128]{2,1,0:T(8,128)S(1)}, f32[32,32,128]{2,1,0:T(8,128)S(1)}, u32[]{:S(2)}, u32[]{:S(2)}) collective-permute-start(f32[32,32,128]{2,1,0:T(8,128)S(1)} %bitcast.22), channel_id=1, source_target_pairs={{0,4},{1,5},{2,6},{3,7},{4,0},{5,1},{6,2},{7,3},{8,12},{9,13},{10,... | collective-permute-start | bytes 1572872 | tf_op jit(solution)/shard_map/ppermute | solution.py:30
  34.6 16.4 %collective-permute-start.5 = (f32[32,32,128]{2,1,0:T(8,128)S(1)}, f32[32,32,128]{2,1,0:T(8,128)S(1)}, u32[]{:S(2)}, u32[]{:S(2)}) collective-permute-start(f32[32,32,128]{2,1,0:T(8,128)S(1)} %collective-permute-done.3.refs_4_.refs_5_), channel_id=1, source_target_pairs={{0,64},{1,65},{2,66},{3,67},{4,68},{5,69},{6,70},{7,71},{8,72},{9,... | collective-permute-start | bytes 1572872 | tf_op jit(solution)/shard_map/ppermute | solution.py:30
  35.2 25.7 %collective-permute-start.4 = (f32[32,32,128]{2,1,0:T(8,128)S(1)}, f32[32,32,128]{2,1,0:T(8,128)S(1)}, u32[]{:S(2)}, u32[]{:S(2)}) collective-permute-start(f32[32,32,128]{2,1,0:T(8,128)S(1)} %collective-permute-done.3.refs_4_.refs_5_), channel_id=1, source_target_pairs={{0,192},{1,193},{2,194},{3,195},{4,196},{5,197},{6,198},{7,199},{8... | collective-permute-start | bytes 1572872 | tf_op jit(solution)/shard_map/ppermute | solution.py:30
  44.0 19.9 %collective-permute-start.7 = (f32[32,32,128]{2,1,0:T(8,128)S(1)}, f32[32,32,128]{2,1,0:T(8,128)S(1)}, u32[]{:S(2)}, u32[]{:S(2)}) collective-permute-start(f32[32,32,128]{2,1,0:T(8,128)S(1)} %collective-permute-done.6.refs_3_), channel_id=1, source_target_pairs={{0,24},{1,25},{2,26},{3,27},{4,28},{5,29},{6,30},{7,31},{8,0},{9,1... | collective-permute-start | bytes 1572872 | tf_op jit(solution)/shard_map/ppermute | solution.py:30
  45.8 23.4 %collective-permute-start.12 = (f32[32,32,128]{2,1,0:T(8,128)S(1)}, f32[32,32,128]{2,1,0:T(8,128)S(1)}, u32[]{:S(2)}, u32[]{:S(2)}) collective-permute-start(f32[32,32,128]{2,1,0:T(8,128)S(1)} %collective-permute-done.3.refs_4_.refs_5_), channel_id=1, source_target_pairs={{0,128},{1,129},{2,130},{3,131},{4,132},{5,133},{6,134},{7,135},{8... | collective-permute-start | bytes 1572872 | tf_op jit(solution)/shard_map/ppermute | solution.py:30
  50.8 18.3 %collective-permute-start.10 = (f32[32,32,128]{2,1,0:T(8,128)S(1)}, f32[32,32,128]{2,1,0:T(8,128)S(1)}, u32[]{:S(2)}, u32[]{:S(2)}) collective-permute-start(f32[32,32,128]{2,1,0:T(8,128)S(1)} %collective-permute-done.6.refs_3_), channel_id=1, source_target_pairs={{0,4},{1,5},{2,6},{3,7},{4,0},{5,1},{6,2},{7,3},{8,12},{9,13},{10,... | collective-permute-start | bytes 1572872 | tf_op jit(solution)/shard_map/ppermute | solution.py:30
  63.9 5.3 %collective-permute-start.11 = (f32[32,32,128]{2,1,0:T(8,128)S(1)}, f32[32,32,128]{2,1,0:T(8,128)S(1)}, u32[]{:S(2)}, u32[]{:S(2)}) collective-permute-start(f32[32,32,128]{2,1,0:T(8,128)S(1)} %collective-permute-done.7.refs_3_), channel_id=1, source_target_pairs={{0,4},{1,5},{2,6},{3,7},{4,0},{5,1},{6,2},{7,3},{8,12},{9,13},{10,... | collective-permute-start | bytes 1572872 | tf_op jit(solution)/shard_map/ppermute | solution.py:30
  64.0 14.3 %collective-permute-start.9 = (f32[32,32,128]{2,1,0:T(8,128)S(1)}, f32[32,32,128]{2,1,0:T(8,128)S(1)}, u32[]{:S(2)}, u32[]{:S(2)}) collective-permute-start(f32[32,32,128]{2,1,0:T(8,128)S(1)} %collective-permute-done.7.refs_3_), channel_id=1, source_target_pairs={{0,24},{1,25},{2,26},{3,27},{4,28},{5,29},{6,30},{7,31},{8,0},{9,1... | collective-permute-start | bytes 1572872 | tf_op jit(solution)/shard_map/ppermute | solution.py:30
  78.3 2.2 %collective-permute-start.13 = (f32[32,32,128]{2,1,0:T(8,128)S(1)}, f32[32,32,128]{2,1,0:T(8,128)S(1)}, u32[]{:S(2)}, u32[]{:S(2)}) collective-permute-start(f32[32,32,128]{2,1,0:T(8,128)S(1)} %collective-permute-done.9.refs_3_), channel_id=1, source_target_pairs={{0,4},{1,5},{2,6},{3,7},{4,0},{5,1},{6,2},{7,3},{8,12},{9,13},{10,... | collective-permute-start | bytes 1572872 | tf_op jit(solution)/shard_map/ppermute | solution.py:30
  82.7 8.9 %collective-permute-start.18 = (f32[32,16,128]{2,1,0:T(8,128)S(1)}, f32[32,16,128]{2,1,0:T(8,128)S(1)}, u32[]{:S(2)}, u32[]{:S(2)}) collective-permute-start(f32[32,16,128]{2,1,0:T(8,128)S(1)} %get-tuple-element.69), channel_id=1, source_target_pairs={{0,1},{1,2},{2,3},{3,0},{4,5},{5,6},{6,7},{7,4},{8,9},{9,10},{10,1... | collective-permute-start | bytes 786440 | tf_op jit(solution)/shard_map/ppermute | solution.py:30
  83.3 10.3 %collective-permute-start.19 = (f32[32,16,128]{2,1,0:T(8,128)S(1)}, f32[32,16,128]{2,1,0:T(8,128)S(1)}, u32[]{:S(2)}, u32[]{:S(2)}) collective-permute-start(f32[32,16,128]{2,1,0:T(8,128)S(1)} %get-tuple-element.70), channel_id=1, source_target_pairs={{0,3},{1,0},{2,1},{3,2},{4,7},{5,4},{6,5},{7,6},{8,11},{9,8},{10,9... | collective-permute-start | bytes 786440 | tf_op jit(solution)/shard_map/ppermute | solution.py:30
  87.0 10.3 %collective-permute-start.14 = (f32[32,16,128]{2,1,0:T(8,128)S(1)}, f32[32,16,128]{2,1,0:T(8,128)S(1)}, u32[]{:S(2)}, u32[]{:S(2)}) collective-permute-start(f32[32,16,128]{2,1,0:T(8,128)S(1)} %get-tuple-element.60), channel_id=1, source_target_pairs={{0,1},{1,2},{2,3},{3,0},{4,5},{5,6},{6,7},{7,4},{8,9},{9,10},{10,1... | collective-permute-start | bytes 786440 | tf_op jit(solution)/shard_map/ppermute | solution.py:30
  88.7 10.5 %collective-permute-start.15 = (f32[32,16,128]{2,1,0:T(8,128)S(1)}, f32[32,16,128]{2,1,0:T(8,128)S(1)}, u32[]{:S(2)}, u32[]{:S(2)}) collective-permute-start(f32[32,16,128]{2,1,0:T(8,128)S(1)} %get-tuple-element.61), channel_id=1, source_target_pairs={{0,3},{1,0},{2,1},{3,2},{4,7},{5,4},{6,5},{7,6},{8,11},{9,8},{10,9... | collective-permute-start | bytes 786440 | tf_op jit(solution)/shard_map/ppermute | solution.py:30
  93.6 7.8 %collective-permute-start.20 = (f32[16,16,128]{2,1,0:T(8,128)S(1)}, f32[16,16,128]{2,1,0:T(8,128)S(1)}, u32[]{:S(2)}, u32[]{:S(2)}) collective-permute-start(f32[16,16,128]{2,1,0:T(8,128)S(1)} %slice_add_fusion.1), channel_id=1, source_target_pairs={{0,1},{1,2},{2,3},{3,0},{4,5},{5,6},{6,7},{7,4},{8,9},{9,10},{10,1... | collective-permute-start | bytes 393224 | tf_op jit(solution)/shard_map/ppermute | solution.py:30
  95.4 6.7 %collective-permute-start.21 = (f32[16,16,128]{2,1,0:T(8,128)S(1)}, f32[16,16,128]{2,1,0:T(8,128)S(1)}, u32[]{:S(2)}, u32[]{:S(2)}) collective-permute-start(f32[16,16,128]{2,1,0:T(8,128)S(1)} %slice_add_fusion), channel_id=1, source_target_pairs={{0,3},{1,0},{2,1},{3,2},{4,7},{5,4},{6,5},{7,6},{8,11},{9,8},{10,9... | collective-permute-start | bytes 393224 | tf_op jit(solution)/shard_map/ppermute | solution.py:30
  99.2 5.6 %collective-permute-start.16 = (f32[16,16,128]{2,1,0:T(8,128)S(1)}, f32[16,16,128]{2,1,0:T(8,128)S(1)}, u32[]{:S(2)}, u32[]{:S(2)}) collective-permute-start(f32[16,16,128]{2,1,0:T(8,128)S(1)} %slice_add_fusion.3), channel_id=1, source_target_pairs={{0,1},{1,2},{2,3},{3,0},{4,5},{5,6},{6,7},{7,4},{8,9},{9,10},{10,1... | collective-permute-start | bytes 393224 | tf_op jit(solution)/shard_map/ppermute | solution.py:30
  100.8 6.6 %copy-start.1 = (f32[1,1,32,4096]{3,2,1,0:T(8,128)S(1)}, f32[1,1,32,4096]{3,2,1,0:T(8,128)}, u32[]{:S(2)}) copy-start(f32[1,1,32,4096]{3,2,1,0:T(8,128)} %param.7) | copy-start | bytes 1572868
  100.8 6.3 %collective-permute-start.17 = (f32[16,16,128]{2,1,0:T(8,128)S(1)}, f32[16,16,128]{2,1,0:T(8,128)S(1)}, u32[]{:S(2)}, u32[]{:S(2)}) collective-permute-start(f32[16,16,128]{2,1,0:T(8,128)S(1)} %slice_add_fusion.2), channel_id=1, source_target_pairs={{0,3},{1,0},{2,1},{3,2},{4,7},{5,4},{6,5},{7,6},{8,11},{9,8},{10,9... | collective-permute-start | bytes 393224 | tf_op jit(solution)/shard_map/ppermute | solution.py:30
where the time goes:
time: 108 us
  waiting for transfers between devices  44.8 us (41%)
  starting transfers between devices  33.5 us (31%)
  Pallas kernels  25.4 us (24%)
  local copies, waits for them, and re-layouts  3.11 us (3%)
  other arithmetic  1.17 us (1%)
    ppermute x22, waiting for transfers between devices, moved(): return lax.ppermute(x, AXES, pairs)  44.8 us
    ppermute x22, starting transfers between devices, moved(): return lax.ppermute(x, AXES, pairs)  33.5 us
    pallas_call x8, Pallas kernels, add_sections(): pl.pallas_call(functools.partial(section_kernel, jobs, later, len(lefts),...  25.4 us
    unnamed x7, local copies, waits for them, and re-layouts  3.01 us
  transfers between devices with their start and end apart: 22, of which 13 were waited for; matrix products, arithmetic and copies ran while one was open for 2% of the time, Pallas kernels for 21%

commit v1 on v0

--- a/solution.py
+++ b/solution.py
@@ -230,22 +230,21 @@
     acc, made_even = add_sections(
         [(1, False, 0, [(1, 0)])], *args, [left1], [same1, same3], acc, "sections_b", [even3]
     )
-    near = [(0, 0), (1, 1), (3, 2)]
-    acc = add_sections([(0, True, 0, near)], *args, [twin0], [other0, other1, other3], acc, "sections_c")
     other1, other3, left2, acc = lax.optimization_barrier((other1, other3, left2, acc))
 
     left3 = by_zl(left2, -1)
-    acc = add_sections([(2, False, 0, [(2, 0)])], *args, [left2], [same2], acc, "sections_d")
+    jobs = [(2, False, 1, [(2, 3)]), (0, True, 0, [(0, 0), (1, 1), (3, 2)])]
+    acc = add_sections(jobs, *args, [twin0, left2], [other0, other1, other3, same2], acc, "sections_c")
     twin2 = swap_core(left2)
     other = [other0, other1, other2, other3]
     jobs = [(k, True, k - 1, choices) for k in (1, 2)]
-    acc, made_odd = add_sections(jobs, *args, [twin1, twin2], other, acc, "sections_e", [odd3])
+    acc, made_odd = add_sections(jobs, *args, [twin1, twin2], other, acc, "sections_d", [odd3])
 
     left3, acc = lax.optimization_barrier((left3, acc))
     twin3 = swap_core(left3)
-    acc = add_sections([even3], *args, [left3], [], acc, "sections_f", made=[made_even])
+    acc = add_sections([even3], *args, [left3], [], acc, "sections_e", made=[made_even])
     share = [
-        add_sections([odd3], *args, [twin3], [], acc, f"sections_g{h}", [], h, [made_odd]) for h in range(2)
+        add_sections([odd3], *args, [twin3], [], acc, f"sections_f{h}", [], h, [made_odd]) for h in range(2)
     ]
     share = [reduce_over_depth(half) for half in share]
     share = jnp.concatenate(share, axis=1)

time: 108 us -> 103 us (0.954)
  waiting for transfers between devices: 44.8 us -> 36 us
  starting transfers between devices: 33.5 us -> 37.9 us
    ppermute x22, waiting for transfers between devices: 44.8 us -> 36 us  [moved(): return lax.ppermute(x, AXES, pairs)]
    ppermute x22, starting transfers between devices: 33.5 us -> 37.9 us  [moved(): return lax.ppermute(x, AXES, pairs)]
    pallas_call x8 -> x7, Pallas kernels: 25.4 us -> 24.4 us  [add_sections(): pl.pallas_call(functools.partial(section_kernel, jobs, later, len(lefts),...]
  transfers between devices with their start and end apart: 22 -> 22, of which waited for: 13 -> 13; matrix products, arithmetic and copies ran while one was open for 2% -> 2% of each run, Pallas kernels for 21% -> 22%
where the time goes in v1:
time: 103 us
  starting transfers between devices  37.9 us (37%)
  waiting for transfers between devices  36 us (35%)
  Pallas kernels  24.4 us (24%)
  local copies, waits for them, and re-layouts  3.11 us (3%)
  other arithmetic  1.17 us (1%)
    ppermute x22, starting transfers between devices, moved(): return lax.ppermute(x, AXES, pairs)  37.9 us
    ppermute x22, waiting for transfers between devices, moved(): return lax.ppermute(x, AXES, pairs)  36 us
    pallas_call x7, Pallas kernels, add_sections(): pl.pallas_call(functools.partial(section_kernel, jobs, later, len(lefts),...  24.4 us
    unnamed x7, local copies, waits for them, and re-layouts  3.01 us
  transfers between devices with their start and end apart: 22, of which 13 were waited for; matrix products, arithmetic and copies ran while one was open for 2% of the time, Pallas kernels for 22%

profile of v1, /device:TPU:30, one launch (start us, length us, event | category | flops | bytes accessed | tf_op | source)
XLA Modules:
  0.0 102.8 jit_solution(9450131338745150370)
XLA Ops:
  0.0 1.1 %copy.7 = f32[4,8,32,128]{3,2,1,0:T(8,128)S(1)} copy(f32[4,8,32,128]{3,1,2,0:T(8,128)} %bitcast.37) | data formatting | bytes 1048576
  1.2 7.3 %collective-permute-start.3 = (f32[32,32,128]{2,1,0:T(8,128)S(1)}, f32[32,32,128]{2,1,0:T(8,128)S(1)}, u32[]{:S(2)}, u32[]{:S(2)}) collective-permute-start(f32[32,32,128]{2,1,0:T(8,128)S(1)} %bitcast.15), channel_id=1, source_target_pairs={{0,32},{1,33},{2,34},{3,35},{4,36},{5,37},{6,38},{7,39},{8,40},{9,... | collective-permute-start | bytes 1572872 | tf_op jit(solution)/shard_map/ppermute | solution.py:30
  8.4 1.2 %collective-permute-start.2 = (f32[32,32,128]{2,1,0:T(8,128)S(1)}, f32[32,32,128]{2,1,0:T(8,128)S(1)}, u32[]{:S(2)}, u32[]{:S(2)}) collective-permute-start(f32[32,32,128]{2,1,0:T(8,128)S(1)} %bitcast.16), channel_id=1, source_target_pairs={{0,128},{1,129},{2,130},{3,131},{4,132},{5,133},{6,134},{7,135},{8... | collective-permute-start | bytes 1572872 | tf_op jit(solution)/shard_map/ppermute | solution.py:30
  9.7 2.2 %collective-permute-start.1 = (f32[32,32,128]{2,1,0:T(8,128)S(1)}, f32[32,32,128]{2,1,0:T(8,128)S(1)}, u32[]{:S(2)}, u32[]{:S(2)}) collective-permute-start(f32[32,32,128]{2,1,0:T(8,128)S(1)} %bitcast.17), channel_id=1, source_target_pairs={{0,64},{1,65},{2,66},{3,67},{4,68},{5,69},{6,70},{7,71},{8,72},{9,... | collective-permute-start | bytes 1572872 | tf_op jit(solution)/shard_map/ppermute | solution.py:30
  11.9 0.7 copy.10
  12.6 0.1 pad_add_fusion.refs_0_
  12.6 1.1 %copy.8 = f32[4,8,32,128]{3,2,1,0:T(8,128)S(1)} copy(f32[4,8,32,128]{3,1,2,0:T(8,128)} %bitcast.38) | data formatting | bytes 1048576
  13.8 3.0 %sections_a.1.refs_6_ = f32[129,32,128]{2,1,0:T(8,128)S(1)} custom-call(s32[3]{0:T(128)S(1)} %pad_add_fusion.refs_0_, s32[8,3,64]{2,1,0:T(4,128)S(1)} %bitcast.23, s32[8]{0:T(128)S(1)} %bitcast.30, f32[32,32,128]{2,1,0:T(8,128)S(1)} %bitcast.20, f32[32,32,128]{2,1,0:T(8,128)S(1)} %bitcast.19), custom_call_target="tpu_custom_call" | custom-call | tf_op jit(solution)/shard_map/sections_a/pallas_call | solution.py:182
  16.8 5.9 %collective-permute-done.3.refs_5_ = f32[32,32,128]{2,1,0:T(8,128)S(1)} collective-permute-done((f32[32,32,128]{2,1,0:T(8,128)S(1)}, f32[32,32,128]{2,1,0:T(8,128)S(1)}, u32[]{:S(2)}, u32[]{:S(2)}) %collective-permute-start.3) | collective-permute-done | bytes 524320 | tf_op jit(solution)/shard_map/ppermute | solution.py:30
  22.6 7.0 %collective-permute-start.6 = (f32[32,32,128]{2,1,0:T(8,128)S(1)}, f32[32,32,128]{2,1,0:T(8,128)S(1)}, u32[]{:S(2)}, u32[]{:S(2)}) collective-permute-start(f32[32,32,128]{2,1,0:T(8,128)S(1)} %bitcast.21), channel_id=1, source_target_pairs={{0,24},{1,25},{2,26},{3,27},{4,28},{5,29},{6,30},{7,31},{8,0},{9,1... | collective-permute-start | bytes 1572872 | tf_op jit(solution)/shard_map/ppermute | solution.py:30
  29.6 2.5 %collective-permute-done.1.refs_5_ = f32[32,32,128]{2,1,0:T(8,128)S(1)} collective-permute-done((f32[32,32,128]{2,1,0:T(8,128)S(1)}, f32[32,32,128]{2,1,0:T(8,128)S(1)}, u32[]{:S(2)}, u32[]{:S(2)}) %collective-permute-start.1) | collective-permute-done | bytes 524320 | tf_op jit(solution)/shard_map/ppermute | solution.py:30
  32.1 2.4 %collective-permute-done.refs_4_ = f32[32,32,128]{2,1,0:T(8,128)S(1)} collective-permute-done((f32[32,32,128]{2,1,0:T(8,128)S(1)}, f32[32,32,128]{2,1,0:T(8,128)S(1)}, u32[]{:S(2)}, u32[]{:S(2)}) %collective-permute-start) | collective-permute-done | bytes 524320 | tf_op jit(solution)/shard_map/ppermute | solution.py:30
  34.6 0.6 collective-permute-start.5
  35.2 1.4 %collective-permute-start.4 = (f32[32,32,128]{2,1,0:T(8,128)S(1)}, f32[32,32,128]{2,1,0:T(8,128)S(1)}, u32[]{:S(2)}, u32[]{:S(2)}) collective-permute-start(f32[32,32,128]{2,1,0:T(8,128)S(1)} %collective-permute-done.3.refs_5_), channel_id=1, source_target_pairs={{0,192},{1,193},{2,194},{3,195},{4,196},{5,197},{6,198},{7,199},{8... | collective-permute-start | bytes 1572872 | tf_op jit(solution)/shard_map/ppermute | solution.py:30
  36.6 7.4 %collective-permute-done.6.refs_3_ = f32[32,32,128]{2,1,0:T(8,128)S(1)} collective-permute-done((f32[32,32,128]{2,1,0:T(8,128)S(1)}, f32[32,32,128]{2,1,0:T(8,128)S(1)}, u32[]{:S(2)}, u32[]{:S(2)}) %collective-permute-start.6) | collective-permute-done | bytes 524320 | tf_op jit(solution)/shard_map/ppermute | solution.py:30
  44.0 1.8 %collective-permute-start.7 = (f32[32,32,128]{2,1,0:T(8,128)S(1)}, f32[32,32,128]{2,1,0:T(8,128)S(1)}, u32[]{:S(2)}, u32[]{:S(2)}) collective-permute-start(f32[32,32,128]{2,1,0:T(8,128)S(1)} %collective-permute-done.6.refs_3_), channel_id=1, source_target_pairs={{0,24},{1,25},{2,26},{3,27},{4,28},{5,29},{6,30},{7,31},{8,0},{9,1... | collective-permute-start | bytes 1572872 | tf_op jit(solution)/shard_map/ppermute | solution.py:30
  45.8 1.2 %collective-permute-start.11 = (f32[32,32,128]{2,1,0:T(8,128)S(1)}, f32[32,32,128]{2,1,0:T(8,128)S(1)}, u32[]{:S(2)}, u32[]{:S(2)}) collective-permute-start(f32[32,32,128]{2,1,0:T(8,128)S(1)} %collective-permute-done.3.refs_5_), channel_id=1, source_target_pairs={{0,128},{1,129},{2,130},{3,131},{4,132},{5,133},{6,134},{7,135},{8... | collective-permute-start | bytes 1572872 | tf_op jit(solution)/shard_map/ppermute | solution.py:30
  47.0 3.8 %sections_b.1 = (f32[129,32,128]{2,1,0:T(8,128)S(1)}, bf16[32,128,128]{2,1,0:T(8,128)(2,1)S(1)}) custom-call(s32[3]{0:T(128)S(1)} %pad_add_fusion.refs_0_, s32[8,3,64]{2,1,0:T(4,128)S(1)} %bitcast.24, s32[8]{0:T(128)S(1)} %bitcast.31, f32[32,32,128]{2,1,0:T(8,128)S(1)} %collective-permute-done.6.refs_3_, f32[32,32,128]{2,1,0:T(8,128)S(1)} %collective-permute-done.refs_4_, ...), custom_call_target="tpu_custom_call" | custom-call | tf_op jit(solution)/shard_map/sections_b/pallas_call | solution.py:182
  50.8 0.8 collective-permute-start.9
  51.6 5.0 %collective-permute-done.7.refs_4_ = f32[32,32,128]{2,1,0:T(8,128)S(1)} collective-permute-done((f32[32,32,128]{2,1,0:T(8,128)S(1)}, f32[32,32,128]{2,1,0:T(8,128)S(1)}, u32[]{:S(2)}, u32[]{:S(2)}) %collective-permute-start.7) | collective-permute-done | bytes 524320 | tf_op jit(solution)/shard_map/ppermute | solution.py:30
  56.6 4.3 %collective-permute-start.8 = (f32[32,32,128]{2,1,0:T(8,128)S(1)}, f32[32,32,128]{2,1,0:T(8,128)S(1)}, u32[]{:S(2)}, u32[]{:S(2)}) collective-permute-start(f32[32,32,128]{2,1,0:T(8,128)S(1)} %collective-permute-done.7.refs_4_), channel_id=1, source_target_pairs={{0,24},{1,25},{2,26},{3,27},{4,28},{5,29},{6,30},{7,31},{8,0},{9,1... | collective-permute-start | bytes 1572872 | tf_op jit(solution)/shard_map/ppermute | solution.py:30
  60.9 5.1 %sections_c.1.refs_9_ = f32[129,32,128]{2,1,0:T(8,128)S(1)} custom-call(s32[3]{0:T(128)S(1)} %pad_add_fusion.refs_0_, s32[8,3,64]{2,1,0:T(4,128)S(1)} %bitcast.25, s32[8]{0:T(128)S(1)} %bitcast.32, f32[32,32,128]{2,1,0:T(8,128)S(1)} %collective-permute-done.12.refs_3_, f32[32,32,128]{2,1,0:T(8,128)S(1)} %collective-permute-done.7.refs_4_, ...), custom_call_target="tpu_custom_call" | custom-call | tf_op jit(solution)/shard_map/sections_c/pallas_call | solution.py:182
  66.0 6.1 %sections_d.1 = (f32[129,32,128]{2,1,0:T(8,128)S(1)}, bf16[32,128,128]{2,1,0:T(8,128)(2,1)S(1)}) custom-call(s32[3]{0:T(128)S(1)} %pad_add_fusion.refs_0_, s32[8,3,64]{2,1,0:T(4,128)S(1)} %bitcast.26, s32[8]{0:T(128)S(1)} %bitcast.33, f32[32,32,128]{2,1,0:T(8,128)S(1)} %collective-permute-done.9.refs_3_, f32[32,32,128]{2,1,0:T(8,128)S(1)} %collective-permute-done.10.refs_4_, ...), custom_call_target="tpu_custom_call" | custom-call | tf_op jit(solution)/shard_map/sections_d/pallas_call | solution.py:182
  72.1 0.6 collective-permute-done.8.refs_3_
  72.7 1.5 %collective-permute-start.13 = (f32[32,32,128]{2,1,0:T(8,128)S(1)}, f32[32,32,128]{2,1,0:T(8,128)S(1)}, u32[]{:S(2)}, u32[]{:S(2)}) collective-permute-start(f32[32,32,128]{2,1,0:T(8,128)S(1)} %collective-permute-done.8.refs_3_), channel_id=1, source_target_pairs={{0,4},{1,5},{2,6},{3,7},{4,0},{5,1},{6,2},{7,3},{8,12},{9,13},{10,... | collective-permute-start | bytes 1572872 | tf_op jit(solution)/shard_map/ppermute | solution.py:30
  74.3 2.2 %sections_e.1.refs_5_ = f32[129,32,128]{2,1,0:T(8,128)S(1)} custom-call(s32[3]{0:T(128)S(1)} %pad_add_fusion.refs_0_, s32[8,3,64]{2,1,0:T(4,128)S(1)} %bitcast.27, s32[8]{0:T(128)S(1)} %bitcast.34, f32[32,32,128]{2,1,0:T(8,128)S(1)} %collective-permute-done.8.refs_3_, bf16[32,128,128]{2,1,0:T(8,128)(2,1)S(1)} %get-tuple-element.57.refs_4_, ...), custom_call_target="tpu_custom_call" | custom-call | tf_op jit(solution)/shard_map/sections_e/pallas_call | solution.py:182
  76.5 2.1 %sections_f1.1 = (f32[32,16,128]{2,1,0:T(8,128)S(1)}, f32[16,16,128]{2,1,0:T(8,128)S(1)}, f32[32,16,128]{2,1,0:T(8,128)S(1)}, f32[32,16,128]{2,1,0:T(8,128)S(1)}, f32[16,16,128]{2,1,0:T(8,128)S(1)}) custom-call(s32[3]{0:T(128)S(1)} %pad_add_fusion.refs_0_, s32[8,3,64]{2,1,0:T(4,128)S(1)} %bitcast.28, s32[8]{0:T(128)S(1)} %bitcast.35, ...), custom_call_target="tpu_custom_call" | custom-call | tf_op jit(solution)/shard_map/sections_f1/pallas_call | solution.py:182
  78.6 0.1 collective-permute-start.18
  78.7 2.0 %collective-permute-start.19 = (f32[32,16,128]{2,1,0:T(8,128)S(1)}, f32[32,16,128]{2,1,0:T(8,128)S(1)}, u32[]{:S(2)}, u32[]{:S(2)}) collective-permute-start(f32[32,16,128]{2,1,0:T(8,128)S(1)} %get-tuple-element.70), channel_id=1, source_target_pairs={{0,3},{1,0},{2,1},{3,2},{4,7},{5,4},{6,5},{7,6},{8,11},{9,8},{10,9... | collective-permute-start | bytes 786440 | tf_op jit(solution)/shard_map/ppermute | solution.py:30
  80.7 2.1 %sections_f0.1 = (f32[32,16,128]{2,1,0:T(8,128)S(1)}, f32[16,16,128]{2,1,0:T(8,128)S(1)}, f32[32,16,128]{2,1,0:T(8,128)S(1)}, f32[32,16,128]{2,1,0:T(8,128)S(1)}, f32[16,16,128]{2,1,0:T(8,128)S(1)}) custom-call(s32[3]{0:T(128)S(1)} %pad_add_fusion.refs_0_, s32[8,3,64]{2,1,0:T(4,128)S(1)} %bitcast.29, s32[8]{0:T(128)S(1)} %bitcast.36, ...), custom_call_target="tpu_custom_call" | custom-call | tf_op jit(solution)/shard_map/sections_f0/pallas_call | solution.py:182
  82.9 1.4 %collective-permute-start.14 = (f32[32,16,128]{2,1,0:T(8,128)S(1)}, f32[32,16,128]{2,1,0:T(8,128)S(1)}, u32[]{:S(2)}, u32[]{:S(2)}) collective-permute-start(f32[32,16,128]{2,1,0:T(8,128)S(1)} %get-tuple-element.60), channel_id=1, source_target_pairs={{0,1},{1,2},{2,3},{3,0},{4,5},{5,6},{6,7},{7,4},{8,9},{9,10},{10,1... | collective-permute-start | bytes 786440 | tf_op jit(solution)/shard_map/ppermute | solution.py:30
  84.2 0.7 collective-permute-start.15
  85.0 2.9 %collective-permute-done.18 = f32[32,16,128]{2,1,0:T(8,128)S(1)} collective-permute-done((f32[32,16,128]{2,1,0:T(8,128)S(1)}, f32[32,16,128]{2,1,0:T(8,128)S(1)}, u32[]{:S(2)}, u32[]{:S(2)}) %collective-permute-start.18) | collective-permute-done | bytes 262176 | tf_op jit(solution)/shard_map/ppermute | solution.py:30
  87.9 1.3 %collective-permute-done.19 = f32[32,16,128]{2,1,0:T(8,128)S(1)} collective-permute-done((f32[32,16,128]{2,1,0:T(8,128)S(1)}, f32[32,16,128]{2,1,0:T(8,128)S(1)}, u32[]{:S(2)}, u32[]{:S(2)}) %collective-permute-start.19) | collective-permute-done | bytes 262176 | tf_op jit(solution)/shard_map/ppermute | solution.py:30
  89.2 0.1 collective-permute-start.20
  89.3 2.1 %collective-permute-start.21 = (f32[16,16,128]{2,1,0:T(8,128)S(1)}, f32[16,16,128]{2,1,0:T(8,128)S(1)}, u32[]{:S(2)}, u32[]{:S(2)}) collective-permute-start(f32[16,16,128]{2,1,0:T(8,128)S(1)} %slice_add_fusion), channel_id=1, source_target_pairs={{0,3},{1,0},{2,1},{3,2},{4,7},{5,4},{6,5},{7,6},{8,11},{9,8},{10,9... | collective-permute-start | bytes 393224 | tf_op jit(solution)/shard_map/ppermute | solution.py:30
  91.4 2.1 %collective-permute-done.14 = f32[32,16,128]{2,1,0:T(8,128)S(1)} collective-permute-done((f32[32,16,128]{2,1,0:T(8,128)S(1)}, f32[32,16,128]{2,1,0:T(8,128)S(1)}, u32[]{:S(2)}, u32[]{:S(2)}) %collective-permute-start.14) | collective-permute-done | bytes 262176 | tf_op jit(solution)/shard_map/ppermute | solution.py:30
  93.5 1.3 %collective-permute-done.15 = f32[32,16,128]{2,1,0:T(8,128)S(1)} collective-permute-done((f32[32,16,128]{2,1,0:T(8,128)S(1)}, f32[32,16,128]{2,1,0:T(8,128)S(1)}, u32[]{:S(2)}, u32[]{:S(2)}) %collective-permute-start.15) | collective-permute-done | bytes 262176 | tf_op jit(solution)/shard_map/ppermute | solution.py:30
  94.8 0.1 collective-permute-start.16
  94.9 0.0 copy-start.1
  94.9 2.1 %collective-permute-start.17 = (f32[16,16,128]{2,1,0:T(8,128)S(1)}, f32[16,16,128]{2,1,0:T(8,128)S(1)}, u32[]{:S(2)}, u32[]{:S(2)}) collective-permute-start(f32[16,16,128]{2,1,0:T(8,128)S(1)} %slice_add_fusion.2), channel_id=1, source_target_pairs={{0,3},{1,0},{2,1},{3,2},{4,7},{5,4},{6,5},{7,6},{8,11},{9,8},{10,9... | collective-permute-start | bytes 393224 | tf_op jit(solution)/shard_map/ppermute | solution.py:30
  97.0 0.5 collective-permute-done.21
  97.5 2.7 %collective-permute-done.16 = f32[16,16,128]{2,1,0:T(8,128)S(1)} collective-permute-done((f32[16,16,128]{2,1,0:T(8,128)S(1)}, f32[16,16,128]{2,1,0:T(8,128)S(1)}, u32[]{:S(2)}, u32[]{:S(2)}) %collective-permute-start.16) | collective-permute-done | bytes 131104 | tf_op jit(solution)/shard_map/ppermute | solution.py:30
  100.3 1.3 %collective-permute-done.17 = f32[16,16,128]{2,1,0:T(8,128)S(1)} collective-permute-done((f32[16,16,128]{2,1,0:T(8,128)S(1)}, f32[16,16,128]{2,1,0:T(8,128)S(1)}, u32[]{:S(2)}, u32[]{:S(2)}) %collective-permute-start.17) | collective-permute-done | bytes 131104 | tf_op jit(solution)/shard_map/ppermute | solution.py:30
  101.6 0.1 add_add_fusion.1
  101.7 0.1 maximum_multiply_fusion
  101.8 0.1 mul.27
  101.9 0.8 multiply_subtract_fusion
  (19 shorter events, 0.1 us)
Async XLA Ops:
  0.0 13.8 %copy-start = (s32[1,1,1,8]{3,2,1,0:T(1,128)S(1)}, s32[1,1,1,8]{3,2,1,0:T(1,128)}, u32[]{:S(2)}) copy-start(s32[1,1,1,8]{3,2,1,0:T(1,128)} %param.9) | copy-start | bytes 100
  1.2 21.5 %collective-permute-start.3 = (f32[32,32,128]{2,1,0:T(8,128)S(1)}, f32[32,32,128]{2,1,0:T(8,128)S(1)}, u32[]{:S(2)}, u32[]{:S(2)}) collective-permute-start(f32[32,32,128]{2,1,0:T(8,128)S(1)} %bitcast.15), channel_id=1, source_target_pairs={{0,32},{1,33},{2,34},{3,35},{4,36},{5,37},{6,38},{7,39},{8,40},{9,... | collective-permute-start | bytes 1572872 | tf_op jit(solution)/shard_map/ppermute | solution.py:30
  8.4 21.2 %collective-permute-start.2 = (f32[32,32,128]{2,1,0:T(8,128)S(1)}, f32[32,32,128]{2,1,0:T(8,128)S(1)}, u32[]{:S(2)}, u32[]{:S(2)}) collective-permute-start(f32[32,32,128]{2,1,0:T(8,128)S(1)} %bitcast.16), channel_id=1, source_target_pairs={{0,128},{1,129},{2,130},{3,131},{4,132},{5,133},{6,134},{7,135},{8... | collective-permute-start | bytes 1572872 | tf_op jit(solution)/shard_map/ppermute | solution.py:30
  9.7 22.5 %collective-permute-start.1 = (f32[32,32,128]{2,1,0:T(8,128)S(1)}, f32[32,32,128]{2,1,0:T(8,128)S(1)}, u32[]{:S(2)}, u32[]{:S(2)}) collective-permute-start(f32[32,32,128]{2,1,0:T(8,128)S(1)} %bitcast.17), channel_id=1, source_target_pairs={{0,64},{1,65},{2,66},{3,67},{4,68},{5,69},{6,70},{7,71},{8,72},{9,... | collective-permute-start | bytes 1572872 | tf_op jit(solution)/shard_map/ppermute | solution.py:30
  11.8 22.7 %collective-permute-start = (f32[32,32,128]{2,1,0:T(8,128)S(1)}, f32[32,32,128]{2,1,0:T(8,128)S(1)}, u32[]{:S(2)}, u32[]{:S(2)}) collective-permute-start(f32[32,32,128]{2,1,0:T(8,128)S(1)} %bitcast.18), channel_id=1, source_target_pairs={{0,192},{1,193},{2,194},{3,195},{4,196},{5,197},{6,198},{7,199},{8... | collective-permute-start | bytes 1572872 | tf_op jit(solution)/shard_map/ppermute | solution.py:30
  22.6 21.4 %collective-permute-start.6 = (f32[32,32,128]{2,1,0:T(8,128)S(1)}, f32[32,32,128]{2,1,0:T(8,128)S(1)}, u32[]{:S(2)}, u32[]{:S(2)}) collective-permute-start(f32[32,32,128]{2,1,0:T(8,128)S(1)} %bitcast.21), channel_id=1, source_target_pairs={{0,24},{1,25},{2,26},{3,27},{4,28},{5,29},{6,30},{7,31},{8,0},{9,1... | collective-permute-start | bytes 1572872 | tf_op jit(solution)/shard_map/ppermute | solution.py:30
  34.6 16.3 %collective-permute-start.5 = (f32[32,32,128]{2,1,0:T(8,128)S(1)}, f32[32,32,128]{2,1,0:T(8,128)S(1)}, u32[]{:S(2)}, u32[]{:S(2)}) collective-permute-start(f32[32,32,128]{2,1,0:T(8,128)S(1)} %collective-permute-done.3.refs_5_), channel_id=1, source_target_pairs={{0,64},{1,65},{2,66},{3,67},{4,68},{5,69},{6,70},{7,71},{8,72},{9,... | collective-permute-start | bytes 1572872 | tf_op jit(solution)/shard_map/ppermute | solution.py:30
  35.2 16.4 %collective-permute-start.4 = (f32[32,32,128]{2,1,0:T(8,128)S(1)}, f32[32,32,128]{2,1,0:T(8,128)S(1)}, u32[]{:S(2)}, u32[]{:S(2)}) collective-permute-start(f32[32,32,128]{2,1,0:T(8,128)S(1)} %collective-permute-done.3.refs_5_), channel_id=1, source_target_pairs={{0,192},{1,193},{2,194},{3,195},{4,196},{5,197},{6,198},{7,199},{8... | collective-permute-start | bytes 1572872 | tf_op jit(solution)/shard_map/ppermute | solution.py:30
  44.0 12.6 %collective-permute-start.7 = (f32[32,32,128]{2,1,0:T(8,128)S(1)}, f32[32,32,128]{2,1,0:T(8,128)S(1)}, u32[]{:S(2)}, u32[]{:S(2)}) collective-permute-start(f32[32,32,128]{2,1,0:T(8,128)S(1)} %collective-permute-done.6.refs_3_), channel_id=1, source_target_pairs={{0,24},{1,25},{2,26},{3,27},{4,28},{5,29},{6,30},{7,31},{8,0},{9,1... | collective-permute-start | bytes 1572872 | tf_op jit(solution)/shard_map/ppermute | solution.py:30
  45.8 15.1 %collective-permute-start.12 = (f32[32,32,128]{2,1,0:T(8,128)S(1)}, f32[32,32,128]{2,1,0:T(8,128)S(1)}, u32[]{:S(2)}, u32[]{:S(2)}) collective-permute-start(f32[32,32,128]{2,1,0:T(8,128)S(1)} %bitcast.22), channel_id=1, source_target_pairs={{0,4},{1,5},{2,6},{3,7},{4,0},{5,1},{6,2},{7,3},{8,12},{9,13},{10,... | collective-permute-start | bytes 1572872 | tf_op jit(solution)/shard_map/ppermute | solution.py:30
  45.8 20.2 %collective-permute-start.11 = (f32[32,32,128]{2,1,0:T(8,128)S(1)}, f32[32,32,128]{2,1,0:T(8,128)S(1)}, u32[]{:S(2)}, u32[]{:S(2)}) collective-permute-start(f32[32,32,128]{2,1,0:T(8,128)S(1)} %collective-permute-done.3.refs_5_), channel_id=1, source_target_pairs={{0,128},{1,129},{2,130},{3,131},{4,132},{5,133},{6,134},{7,135},{8... | collective-permute-start | bytes 1572872 | tf_op jit(solution)/shard_map/ppermute | solution.py:30
  50.8 15.1 %collective-permute-start.9 = (f32[32,32,128]{2,1,0:T(8,128)S(1)}, f32[32,32,128]{2,1,0:T(8,128)S(1)}, u32[]{:S(2)}, u32[]{:S(2)}) collective-permute-start(f32[32,32,128]{2,1,0:T(8,128)S(1)} %collective-permute-done.6.refs_3_), channel_id=1, source_target_pairs={{0,4},{1,5},{2,6},{3,7},{4,0},{5,1},{6,2},{7,3},{8,12},{9,13},{10,... | collective-permute-start | bytes 1572872 | tf_op jit(solution)/shard_map/ppermute | solution.py:30
  56.6 9.4 %collective-permute-start.10 = (f32[32,32,128]{2,1,0:T(8,128)S(1)}, f32[32,32,128]{2,1,0:T(8,128)S(1)}, u32[]{:S(2)}, u32[]{:S(2)}) collective-permute-start(f32[32,32,128]{2,1,0:T(8,128)S(1)} %collective-permute-done.7.refs_4_), channel_id=1, source_target_pairs={{0,4},{1,5},{2,6},{3,7},{4,0},{5,1},{6,2},{7,3},{8,12},{9,13},{10,... | collective-permute-start | bytes 1572872 | tf_op jit(solution)/shard_map/ppermute | solution.py:30
  56.6 16.1 %collective-permute-start.8 = (f32[32,32,128]{2,1,0:T(8,128)S(1)}, f32[32,32,128]{2,1,0:T(8,128)S(1)}, u32[]{:S(2)}, u32[]{:S(2)}) collective-permute-start(f32[32,32,128]{2,1,0:T(8,128)S(1)} %collective-permute-done.7.refs_4_), channel_id=1, source_target_pairs={{0,24},{1,25},{2,26},{3,27},{4,28},{5,29},{6,30},{7,31},{8,0},{9,1... | collective-permute-start | bytes 1572872 | tf_op jit(solution)/shard_map/ppermute | solution.py:30
  72.7 3.7 %collective-permute-start.13 = (f32[32,32,128]{2,1,0:T(8,128)S(1)}, f32[32,32,128]{2,1,0:T(8,128)S(1)}, u32[]{:S(2)}, u32[]{:S(2)}) collective-permute-start(f32[32,32,128]{2,1,0:T(8,128)S(1)} %collective-permute-done.8.refs_3_), channel_id=1, source_target_pairs={{0,4},{1,5},{2,6},{3,7},{4,0},{5,1},{6,2},{7,3},{8,12},{9,13},{10,... | collective-permute-start | bytes 1572872 | tf_op jit(solution)/shard_map/ppermute | solution.py:30
  78.6 9.3 %collective-permute-start.18 = (f32[32,16,128]{2,1,0:T(8,128)S(1)}, f32[32,16,128]{2,1,0:T(8,128)S(1)}, u32[]{:S(2)}, u32[]{:S(2)}) collective-permute-start(f32[32,16,128]{2,1,0:T(8,128)S(1)} %get-tuple-element.69), channel_id=1, source_target_pairs={{0,1},{1,2},{2,3},{3,0},{4,5},{5,6},{6,7},{7,4},{8,9},{9,10},{10,1... | collective-permute-start | bytes 786440 | tf_op jit(solution)/shard_map/ppermute | solution.py:30
  78.7 10.5 %collective-permute-start.19 = (f32[32,16,128]{2,1,0:T(8,128)S(1)}, f32[32,16,128]{2,1,0:T(8,128)S(1)}, u32[]{:S(2)}, u32[]{:S(2)}) collective-permute-start(f32[32,16,128]{2,1,0:T(8,128)S(1)} %get-tuple-element.70), channel_id=1, source_target_pairs={{0,3},{1,0},{2,1},{3,2},{4,7},{5,4},{6,5},{7,6},{8,11},{9,8},{10,9... | collective-permute-start | bytes 786440 | tf_op jit(solution)/shard_map/ppermute | solution.py:30
  82.9 10.6 %collective-permute-start.14 = (f32[32,16,128]{2,1,0:T(8,128)S(1)}, f32[32,16,128]{2,1,0:T(8,128)S(1)}, u32[]{:S(2)}, u32[]{:S(2)}) collective-permute-start(f32[32,16,128]{2,1,0:T(8,128)S(1)} %get-tuple-element.60), channel_id=1, source_target_pairs={{0,1},{1,2},{2,3},{3,0},{4,5},{5,6},{6,7},{7,4},{8,9},{9,10},{10,1... | collective-permute-start | bytes 786440 | tf_op jit(solution)/shard_map/ppermute | solution.py:30
  84.2 10.6 %collective-permute-start.15 = (f32[32,16,128]{2,1,0:T(8,128)S(1)}, f32[32,16,128]{2,1,0:T(8,128)S(1)}, u32[]{:S(2)}, u32[]{:S(2)}) collective-permute-start(f32[32,16,128]{2,1,0:T(8,128)S(1)} %get-tuple-element.61), channel_id=1, source_target_pairs={{0,3},{1,0},{2,1},{3,2},{4,7},{5,4},{6,5},{7,6},{8,11},{9,8},{10,9... | collective-permute-start | bytes 786440 | tf_op jit(solution)/shard_map/ppermute | solution.py:30
  89.2 7.8 %collective-permute-start.20 = (f32[16,16,128]{2,1,0:T(8,128)S(1)}, f32[16,16,128]{2,1,0:T(8,128)S(1)}, u32[]{:S(2)}, u32[]{:S(2)}) collective-permute-start(f32[16,16,128]{2,1,0:T(8,128)S(1)} %slice_add_fusion.1), channel_id=1, source_target_pairs={{0,1},{1,2},{2,3},{3,0},{4,5},{5,6},{6,7},{7,4},{8,9},{9,10},{10,1... | collective-permute-start | bytes 393224 | tf_op jit(solution)/shard_map/ppermute | solution.py:30
  89.3 8.2 %collective-permute-start.21 = (f32[16,16,128]{2,1,0:T(8,128)S(1)}, f32[16,16,128]{2,1,0:T(8,128)S(1)}, u32[]{:S(2)}, u32[]{:S(2)}) collective-permute-start(f32[16,16,128]{2,1,0:T(8,128)S(1)} %slice_add_fusion), channel_id=1, source_target_pairs={{0,3},{1,0},{2,1},{3,2},{4,7},{5,4},{6,5},{7,6},{8,11},{9,8},{10,9... | collective-permute-start | bytes 393224 | tf_op jit(solution)/shard_map/ppermute | solution.py:30
  94.8 5.5 %collective-permute-start.16 = (f32[16,16,128]{2,1,0:T(8,128)S(1)}, f32[16,16,128]{2,1,0:T(8,128)S(1)}, u32[]{:S(2)}, u32[]{:S(2)}) collective-permute-start(f32[16,16,128]{2,1,0:T(8,128)S(1)} %slice_add_fusion.3), channel_id=1, source_target_pairs={{0,1},{1,2},{2,3},{3,0},{4,5},{5,6},{6,7},{7,4},{8,9},{9,10},{10,1... | collective-permute-start | bytes 393224 | tf_op jit(solution)/shard_map/ppermute | solution.py:30
  94.9 7.0 %copy-start.1 = (f32[1,1,32,4096]{3,2,1,0:T(8,128)S(1)}, f32[1,1,32,4096]{3,2,1,0:T(8,128)}, u32[]{:S(2)}) copy-start(f32[1,1,32,4096]{3,2,1,0:T(8,128)} %param.7) | copy-start | bytes 1572868
  94.9 6.7 %collective-permute-start.17 = (f32[16,16,128]{2,1,0:T(8,128)S(1)}, f32[16,16,128]{2,1,0:T(8,128)S(1)}, u32[]{:S(2)}, u32[]{:S(2)}) collective-permute-start(f32[16,16,128]{2,1,0:T(8,128)S(1)} %slice_add_fusion.2), channel_id=1, source_target_pairs={{0,3},{1,0},{2,1},{3,2},{4,7},{5,4},{6,5},{7,6},{8,11},{9,8},{10,9... | collective-permute-start | bytes 393224 | tf_op jit(solution)/shard_map/ppermute | solution.py:30

commit v2 on v1

--- a/solution.py
+++ b/solution.py
@@ -220,19 +220,21 @@
     twin0 = swap_core(left)
     acc = add_sections([(0, False, 0, [(0, 0)])], *args, [left], [right], None, "sections_a")
     other0, acc, left = lax.optimization_barrier((other0, acc, left))
-    left1 = by_zl(left, -1)
+    halves1 = [by_zl(left[16 * i : 16 * i + 16], -1) for i in range(2)]
+    left1 = jnp.concatenate(halves1)
     same1, same3, same2, other0, acc = lax.optimization_barrier((same1, same3, same2, other0, acc))
 
     other1, other3, other2 = by_y(other0, -1), by_y(other0, 1), by_y(other0, 2)
-    left2 = by_zl(left1, -1)
+    halves2 = [by_zl(x, -1) for x in halves1]
     twin1 = swap_core(left1)
     even3, odd3 = (3, False, 0, [(3, 1)]), (3, True, 0, choices)
     acc, made_even = add_sections(
         [(1, False, 0, [(1, 0)])], *args, [left1], [same1, same3], acc, "sections_b", [even3]
     )
-    other1, other3, left2, acc = lax.optimization_barrier((other1, other3, left2, acc))
-
-    left3 = by_zl(left2, -1)
+    other1, other3, acc, *halves2 = lax.optimization_barrier((other1, other3, acc, *halves2))
+    left2 = jnp.concatenate(halves2)
+
+    halves3 = [by_zl(x, -1) for x in halves2]
     jobs = [(2, False, 1, [(2, 3)]), (0, True, 0, [(0, 0), (1, 1), (3, 2)])]
     acc = add_sections(jobs, *args, [twin0, left2], [other0, other1, other3, same2], acc, "sections_c")
     twin2 = swap_core(left2)
@@ -240,7 +242,8 @@
     jobs = [(k, True, k - 1, choices) for k in (1, 2)]
     acc, made_odd = add_sections(jobs, *args, [twin1, twin2], other, acc, "sections_d", [odd3])
 
-    left3, acc = lax.optimization_barrier((left3, acc))
+    halves3[0], halves3[1], acc = lax.optimization_barrier((halves3[0], halves3[1], acc))
+    left3 = jnp.concatenate(halves3)
     twin3 = swap_core(left3)
     acc = add_sections([even3], *args, [left3], [], acc, "sections_e", made=[made_even])
     share = [

time: 103 us -> 104 us (level)
  starting transfers between devices: 37.9 us -> 44.2 us
  waiting for transfers between devices: 36 us -> 29.9 us
    ppermute x22 -> x25, starting transfers between devices: 37.9 us -> 44.2 us  [moved(): return lax.ppermute(x, AXES, pairs)]
    ppermute x22 -> x25, waiting for transfers between devices: 36 us -> 29.9 us  [moved(): return lax.ppermute(x, AXES, pairs)]
    unnamed x7 -> x10, local copies, waits for them, and re-layouts: 3.01 us -> 3.06 us
  transfers between devices with their start and end apart: 22 -> 25, of which waited for: 13 -> 11; matrix products, arithmetic and copies ran while one was open for 2% -> 2% of each run, Pallas kernels for 22% -> 21%
where the time goes in v2:
time: 104 us; the launch traced here: 103 us
  starting transfers between devices  44.2 us (42%)
  waiting for transfers between devices  29.9 us (29%)
  Pallas kernels  24.3 us (23%)
  local copies, waits for them, and re-layouts  3.26 us (3%)
  other arithmetic  1.18 us (1%)
    ppermute x25, starting transfers between devices, moved(): return lax.ppermute(x, AXES, pairs)  44.2 us
    ppermute x25, waiting for transfers between devices, moved(): return lax.ppermute(x, AXES, pairs)  29.9 us
    pallas_call x7, Pallas kernels, add_sections(): pl.pallas_call(functools.partial(section_kernel, jobs, later, len(lefts),...  24.3 us
    unnamed x10, local copies, waits for them, and re-layouts  3.06 us
  transfers between devices with their start and end apart: 25, of which 11 were waited for; matrix products, arithmetic and copies ran while one was open for 2% of the time, Pallas kernels for 21%

profile of v2, /device:TPU:30, one launch (start us, length us, event | category | flops | bytes accessed | tf_op | source)
XLA Modules:
  0.0 103.1 jit_solution(6082675933051086628)
XLA Ops:
  0.0 1.1 %copy.7 = f32[4,8,32,128]{3,2,1,0:T(8,128)S(1)} copy(f32[4,8,32,128]{3,1,2,0:T(8,128)} %bitcast.37) | data formatting | bytes 1048576
  1.2 7.3 %collective-permute-start.3 = (f32[32,32,128]{2,1,0:T(8,128)S(1)}, f32[32,32,128]{2,1,0:T(8,128)S(1)}, u32[]{:S(2)}, u32[]{:S(2)}) collective-permute-start(f32[32,32,128]{2,1,0:T(8,128)S(1)} %bitcast.18), channel_id=1, source_target_pairs={{0,32},{1,33},{2,34},{3,35},{4,36},{5,37},{6,38},{7,39},{8,40},{9,... | collective-permute-start | bytes 1572872 | tf_op jit(solution)/shard_map/ppermute | solution.py:30
  8.4 1.2 %collective-permute-start.2 = (f32[32,32,128]{2,1,0:T(8,128)S(1)}, f32[32,32,128]{2,1,0:T(8,128)S(1)}, u32[]{:S(2)}, u32[]{:S(2)}) collective-permute-start(f32[32,32,128]{2,1,0:T(8,128)S(1)} %bitcast.19), channel_id=1, source_target_pairs={{0,128},{1,129},{2,130},{3,131},{4,132},{5,133},{6,134},{7,135},{8... | collective-permute-start | bytes 1572872 | tf_op jit(solution)/shard_map/ppermute | solution.py:30
  9.7 2.2 %collective-permute-start.1 = (f32[32,32,128]{2,1,0:T(8,128)S(1)}, f32[32,32,128]{2,1,0:T(8,128)S(1)}, u32[]{:S(2)}, u32[]{:S(2)}) collective-permute-start(f32[32,32,128]{2,1,0:T(8,128)S(1)} %bitcast.20), channel_id=1, source_target_pairs={{0,64},{1,65},{2,66},{3,67},{4,68},{5,69},{6,70},{7,71},{8,72},{9,... | collective-permute-start | bytes 1572872 | tf_op jit(solution)/shard_map/ppermute | solution.py:30
  11.9 0.7 copy.10
  12.6 1.1 %copy.8 = f32[4,8,32,128]{3,2,1,0:T(8,128)S(1)} copy(f32[4,8,32,128]{3,1,2,0:T(8,128)} %bitcast.38) | data formatting | bytes 1048576
  13.7 0.1 pad_add_fusion.refs_0_
  13.8 3.0 %sections_a.1.refs_6_ = f32[129,32,128]{2,1,0:T(8,128)S(1)} custom-call(s32[3]{0:T(128)S(1)} %pad_add_fusion.refs_0_, s32[8,3,64]{2,1,0:T(4,128)S(1)} %bitcast.23, s32[8]{0:T(128)S(1)} %bitcast.30, f32[32,32,128]{2,1,0:T(8,128)S(1)} %bitcast.15, f32[32,32,128]{2,1,0:T(8,128)S(1)} %bitcast.22), custom_call_target="tpu_custom_call" | custom-call | tf_op jit(solution)/shard_map/sections_a/pallas_call | solution.py:182
  16.8 5.8 %collective-permute-done.3.refs_5_ = f32[32,32,128]{2,1,0:T(8,128)S(1)} collective-permute-done((f32[32,32,128]{2,1,0:T(8,128)S(1)}, f32[32,32,128]{2,1,0:T(8,128)S(1)}, u32[]{:S(2)}, u32[]{:S(2)}) %collective-permute-start.3) | collective-permute-done | bytes 524320 | tf_op jit(solution)/shard_map/ppermute | solution.py:30
  22.6 7.1 %collective-permute-start.7 = (f32[16,32,128]{2,1,0:T(8,128)S(1)}, f32[16,32,128]{2,1,0:T(8,128)S(1)}, u32[]{:S(2)}, u32[]{:S(2)}) collective-permute-start(f32[16,32,128]{2,1,0:T(8,128)S(1)} %get-tuple-element.81), channel_id=1, source_target_pairs={{0,24},{1,25},{2,26},{3,27},{4,28},{5,29},{6,30},{7,31},{8,0},{9,1... | collective-permute-start | bytes 786440 | tf_op jit(solution)/shard_map/ppermute | solution.py:30
  29.7 5.3 %collective-permute-start.6 = (f32[16,32,128]{2,1,0:T(8,128)S(1)}, f32[16,32,128]{2,1,0:T(8,128)S(1)}, u32[]{:S(2)}, u32[]{:S(2)}) collective-permute-start(f32[16,32,128]{2,1,0:T(8,128)S(1)} %get-tuple-element.82), channel_id=1, source_target_pairs={{0,24},{1,25},{2,26},{3,27},{4,28},{5,29},{6,30},{7,31},{8,0},{9,1... | collective-permute-start | bytes 786440 | tf_op jit(solution)/shard_map/ppermute | solution.py:30
  35.1 0.3 collective-permute-start.5
  35.4 1.8 %collective-permute-start.4 = (f32[32,32,128]{2,1,0:T(8,128)S(1)}, f32[32,32,128]{2,1,0:T(8,128)S(1)}, u32[]{:S(2)}, u32[]{:S(2)}) collective-permute-start(f32[32,32,128]{2,1,0:T(8,128)S(1)} %collective-permute-done.3.refs_5_), channel_id=1, source_target_pairs={{0,192},{1,193},{2,194},{3,195},{4,196},{5,197},{6,198},{7,199},{8... | collective-permute-start | bytes 1572872 | tf_op jit(solution)/shard_map/ppermute | solution.py:30
  37.2 2.9 %collective-permute-done.7 = f32[16,32,128]{2,1,0:T(8,128)S(1)} collective-permute-done((f32[16,32,128]{2,1,0:T(8,128)S(1)}, f32[16,32,128]{2,1,0:T(8,128)S(1)}, u32[]{:S(2)}, u32[]{:S(2)}) %collective-permute-start.7) | collective-permute-done | bytes 262176 | tf_op jit(solution)/shard_map/ppermute | solution.py:30
  40.1 1.7 %collective-permute-start.9 = (f32[16,32,128]{2,1,0:T(8,128)S(1)}, f32[16,32,128]{2,1,0:T(8,128)S(1)}, u32[]{:S(2)}, u32[]{:S(2)}) collective-permute-start(f32[16,32,128]{2,1,0:T(8,128)S(1)} %collective-permute-done.7), channel_id=1, source_target_pairs={{0,24},{1,25},{2,26},{3,27},{4,28},{5,29},{6,30},{7,31},{8,0},{9,1... | collective-permute-start | bytes 786440 | tf_op jit(solution)/shard_map/ppermute | solution.py:30
  41.8 3.9 %collective-permute-done.6 = f32[16,32,128]{2,1,0:T(8,128)S(1)} collective-permute-done((f32[16,32,128]{2,1,0:T(8,128)S(1)}, f32[16,32,128]{2,1,0:T(8,128)S(1)}, u32[]{:S(2)}, u32[]{:S(2)}) %collective-permute-start.6) | collective-permute-done | bytes 262176 | tf_op jit(solution)/shard_map/ppermute | solution.py:30
  45.7 1.7 %collective-permute-start.8 = (f32[16,32,128]{2,1,0:T(8,128)S(1)}, f32[16,32,128]{2,1,0:T(8,128)S(1)}, u32[]{:S(2)}, u32[]{:S(2)}) collective-permute-start(f32[16,32,128]{2,1,0:T(8,128)S(1)} %collective-permute-done.6), channel_id=1, source_target_pairs={{0,24},{1,25},{2,26},{3,27},{4,28},{5,29},{6,30},{7,31},{8,0},{9,1... | collective-permute-start | bytes 786440 | tf_op jit(solution)/shard_map/ppermute | solution.py:30
  47.5 3.8 %sections_b.1 = (f32[129,32,128]{2,1,0:T(8,128)S(1)}, bf16[32,128,128]{2,1,0:T(8,128)(2,1)S(1)}) custom-call(s32[3]{0:T(128)S(1)} %pad_add_fusion.refs_0_, s32[8,3,64]{2,1,0:T(4,128)S(1)} %bitcast.24, s32[8]{0:T(128)S(1)} %bitcast.31, f32[32,32,128]{2,1,0:T(8,128)S(1)} %constant_dynamic-update-slice_fusion.refs_3_, ...), custom_call_target="tpu_custom_call" | custom-call | tf_op jit(solution)/shard_map/sections_b/pallas_call | solution.py:182
  51.3 0.0 collective-permute-done.9
  51.3 1.3 %collective-permute-start.14 = (f32[32,32,128]{2,1,0:T(8,128)S(1)}, f32[32,32,128]{2,1,0:T(8,128)S(1)}, u32[]{:S(2)}, u32[]{:S(2)}) collective-permute-start(f32[32,32,128]{2,1,0:T(8,128)S(1)} %collective-permute-done.3.refs_5_), channel_id=1, source_target_pairs={{0,128},{1,129},{2,130},{3,131},{4,132},{5,133},{6,134},{7,135},{8... | collective-permute-start | bytes 1572872 | tf_op jit(solution)/shard_map/ppermute | solution.py:30
  52.6 2.7 %collective-permute-done.8 = f32[16,32,128]{2,1,0:T(8,128)S(1)} collective-permute-done((f32[16,32,128]{2,1,0:T(8,128)S(1)}, f32[16,32,128]{2,1,0:T(8,128)S(1)}, u32[]{:S(2)}, u32[]{:S(2)}) %collective-permute-start.8) | collective-permute-done | bytes 262176 | tf_op jit(solution)/shard_map/ppermute | solution.py:30
  55.4 0.6 collective-permute-start.13
  56.0 1.7 %collective-permute-start.10 = (f32[16,32,128]{2,1,0:T(8,128)S(1)}, f32[16,32,128]{2,1,0:T(8,128)S(1)}, u32[]{:S(2)}, u32[]{:S(2)}) collective-permute-start(f32[16,32,128]{2,1,0:T(8,128)S(1)} %collective-permute-done.8), channel_id=1, source_target_pairs={{0,24},{1,25},{2,26},{3,27},{4,28},{5,29},{6,30},{7,31},{8,0},{9,1... | collective-permute-start | bytes 786440 | tf_op jit(solution)/shard_map/ppermute | solution.py:30
  57.7 2.3 %collective-permute-start.11 = (f32[16,32,128]{2,1,0:T(8,128)S(1)}, f32[16,32,128]{2,1,0:T(8,128)S(1)}, u32[]{:S(2)}, u32[]{:S(2)}) collective-permute-start(f32[16,32,128]{2,1,0:T(8,128)S(1)} %collective-permute-done.9), channel_id=1, source_target_pairs={{0,24},{1,25},{2,26},{3,27},{4,28},{5,29},{6,30},{7,31},{8,0},{9,1... | collective-permute-start | bytes 786440 | tf_op jit(solution)/shard_map/ppermute | solution.py:30
  60.0 5.1 %sections_c.1.refs_9_ = f32[129,32,128]{2,1,0:T(8,128)S(1)} custom-call(s32[3]{0:T(128)S(1)} %pad_add_fusion.refs_0_, s32[8,3,64]{2,1,0:T(4,128)S(1)} %bitcast.25, s32[8]{0:T(128)S(1)} %bitcast.32, f32[32,32,128]{2,1,0:T(8,128)S(1)} %collective-permute-done.15.refs_3_, f32[32,32,128]{2,1,0:T(8,128)S(1)} %constant_dynamic-update-slice_fusion.2.refs_4_, ...), custom_call_target="tpu_custom_call" | custom-call | tf_op jit(solution)/shard_map/sections_c/pallas_call | solution.py:182
  65.1 2.2 %collective-permute-done.14.refs_7_ = f32[32,32,128]{2,1,0:T(8,128)S(1)} collective-permute-done((f32[32,32,128]{2,1,0:T(8,128)S(1)}, f32[32,32,128]{2,1,0:T(8,128)S(1)}, u32[]{:S(2)}, u32[]{:S(2)}) %collective-permute-start.14) | collective-permute-done | bytes 524320 | tf_op jit(solution)/shard_map/ppermute | solution.py:30
  67.2 5.9 %sections_d.1 = (f32[129,32,128]{2,1,0:T(8,128)S(1)}, bf16[32,128,128]{2,1,0:T(8,128)(2,1)S(1)}) custom-call(s32[3]{0:T(128)S(1)} %pad_add_fusion.refs_0_, s32[8,3,64]{2,1,0:T(4,128)S(1)} %bitcast.26, s32[8]{0:T(128)S(1)} %bitcast.33, f32[32,32,128]{2,1,0:T(8,128)S(1)} %collective-permute-done.12.refs_3_, ...), custom_call_target="tpu_custom_call" | custom-call | tf_op jit(solution)/shard_map/sections_d/pallas_call | solution.py:182
  73.3 0.1 collective-permute-start.16
  73.4 2.2 %sections_e.1.refs_5_ = f32[129,32,128]{2,1,0:T(8,128)S(1)} custom-call(s32[3]{0:T(128)S(1)} %pad_add_fusion.refs_0_, s32[8,3,64]{2,1,0:T(4,128)S(1)} %bitcast.27, s32[8]{0:T(128)S(1)} %bitcast.34, f32[32,32,128]{2,1,0:T(8,128)S(1)} %constant_dynamic-update-slice_fusion.4.refs_3_, bf16[32,128,128]{2,1,0:T(8,128)(2,1)S(1)} %get-tuple-element.61.refs_4_, ...), custom_call_target="tpu_custom_call" | custom-call | tf_op jit(solution)/shard_map/sections_e/pallas_call | solution.py:182
  75.6 2.1 %sections_f1.1 = (f32[32,16,128]{2,1,0:T(8,128)S(1)}, f32[16,16,128]{2,1,0:T(8,128)S(1)}, f32[32,16,128]{2,1,0:T(8,128)S(1)}, f32[32,16,128]{2,1,0:T(8,128)S(1)}, f32[16,16,128]{2,1,0:T(8,128)S(1)}) custom-call(s32[3]{0:T(128)S(1)} %pad_add_fusion.refs_0_, s32[8,3,64]{2,1,0:T(4,128)S(1)} %bitcast.28, s32[8]{0:T(128)S(1)} %bitcast.35, ...), custom_call_target="tpu_custom_call" | custom-call | tf_op jit(solution)/shard_map/sections_f1/pallas_call | solution.py:182
  77.7 1.4 %collective-permute-start.21 = (f32[32,16,128]{2,1,0:T(8,128)S(1)}, f32[32,16,128]{2,1,0:T(8,128)S(1)}, u32[]{:S(2)}, u32[]{:S(2)}) collective-permute-start(f32[32,16,128]{2,1,0:T(8,128)S(1)} %get-tuple-element.73), channel_id=1, source_target_pairs={{0,1},{1,2},{2,3},{3,0},{4,5},{5,6},{6,7},{7,4},{8,9},{9,10},{10,1... | collective-permute-start | bytes 786440 | tf_op jit(solution)/shard_map/ppermute | solution.py:30
  79.2 0.7 collective-permute-start.22
  79.9 2.1 %sections_f0.1 = (f32[32,16,128]{2,1,0:T(8,128)S(1)}, f32[16,16,128]{2,1,0:T(8,128)S(1)}, f32[32,16,128]{2,1,0:T(8,128)S(1)}, f32[32,16,128]{2,1,0:T(8,128)S(1)}, f32[16,16,128]{2,1,0:T(8,128)S(1)}) custom-call(s32[3]{0:T(128)S(1)} %pad_add_fusion.refs_0_, s32[8,3,64]{2,1,0:T(4,128)S(1)} %bitcast.29, s32[8]{0:T(128)S(1)} %bitcast.36, ...), custom_call_target="tpu_custom_call" | custom-call | tf_op jit(solution)/shard_map/sections_f0/pallas_call | solution.py:182
  82.0 3.1 %collective-permute-start.17 = (f32[32,16,128]{2,1,0:T(8,128)S(1)}, f32[32,16,128]{2,1,0:T(8,128)S(1)}, u32[]{:S(2)}, u32[]{:S(2)}) collective-permute-start(f32[32,16,128]{2,1,0:T(8,128)S(1)} %get-tuple-element.64), channel_id=1, source_target_pairs={{0,1},{1,2},{2,3},{3,0},{4,5},{5,6},{6,7},{7,4},{8,9},{9,10},{10,1... | collective-permute-start | bytes 786440 | tf_op jit(solution)/shard_map/ppermute | solution.py:30
  85.1 1.8 %collective-permute-done.21 = f32[32,16,128]{2,1,0:T(8,128)S(1)} collective-permute-done((f32[32,16,128]{2,1,0:T(8,128)S(1)}, f32[32,16,128]{2,1,0:T(8,128)S(1)}, u32[]{:S(2)}, u32[]{:S(2)}) %collective-permute-start.21) | collective-permute-done | bytes 262176 | tf_op jit(solution)/shard_map/ppermute | solution.py:30
  86.9 2.1 %collective-permute-done.22 = f32[32,16,128]{2,1,0:T(8,128)S(1)} collective-permute-done((f32[32,16,128]{2,1,0:T(8,128)S(1)}, f32[32,16,128]{2,1,0:T(8,128)S(1)}, u32[]{:S(2)}, u32[]{:S(2)}) %collective-permute-start.22) | collective-permute-done | bytes 262176 | tf_op jit(solution)/shard_map/ppermute | solution.py:30
  89.1 0.4 collective-permute-start.23
  89.4 1.8 %collective-permute-start.24 = (f32[16,16,128]{2,1,0:T(8,128)S(1)}, f32[16,16,128]{2,1,0:T(8,128)S(1)}, u32[]{:S(2)}, u32[]{:S(2)}) collective-permute-start(f32[16,16,128]{2,1,0:T(8,128)S(1)} %slice_add_fusion), channel_id=1, source_target_pairs={{0,3},{1,0},{2,1},{3,2},{4,7},{5,4},{6,5},{7,6},{8,11},{9,8},{10,9... | collective-permute-start | bytes 393224 | tf_op jit(solution)/shard_map/ppermute | solution.py:30
  91.3 1.3 %collective-permute-done.17 = f32[32,16,128]{2,1,0:T(8,128)S(1)} collective-permute-done((f32[32,16,128]{2,1,0:T(8,128)S(1)}, f32[32,16,128]{2,1,0:T(8,128)S(1)}, u32[]{:S(2)}, u32[]{:S(2)}) %collective-permute-start.17) | collective-permute-done | bytes 262176 | tf_op jit(solution)/shard_map/ppermute | solution.py:30
  92.6 2.8 %collective-permute-done.18 = f32[32,16,128]{2,1,0:T(8,128)S(1)} collective-permute-done((f32[32,16,128]{2,1,0:T(8,128)S(1)}, f32[32,16,128]{2,1,0:T(8,128)S(1)}, u32[]{:S(2)}, u32[]{:S(2)}) %collective-permute-start.18) | collective-permute-done | bytes 262176 | tf_op jit(solution)/shard_map/ppermute | solution.py:30
  95.4 0.2 collective-permute-start.19
  95.7 1.9 %collective-permute-start.20 = (f32[16,16,128]{2,1,0:T(8,128)S(1)}, f32[16,16,128]{2,1,0:T(8,128)S(1)}, u32[]{:S(2)}, u32[]{:S(2)}) collective-permute-start(f32[16,16,128]{2,1,0:T(8,128)S(1)} %slice_add_fusion.2), channel_id=1, source_target_pairs={{0,3},{1,0},{2,1},{3,2},{4,7},{5,4},{6,5},{7,6},{8,11},{9,8},{10,9... | collective-permute-start | bytes 393224 | tf_op jit(solution)/shard_map/ppermute | solution.py:30
  97.6 2.8 %collective-permute-done.19 = f32[16,16,128]{2,1,0:T(8,128)S(1)} collective-permute-done((f32[16,16,128]{2,1,0:T(8,128)S(1)}, f32[16,16,128]{2,1,0:T(8,128)S(1)}, u32[]{:S(2)}, u32[]{:S(2)}) %collective-permute-start.19) | collective-permute-done | bytes 131104 | tf_op jit(solution)/shard_map/ppermute | solution.py:30
  100.5 1.5 %collective-permute-done.20 = f32[16,16,128]{2,1,0:T(8,128)S(1)} collective-permute-done((f32[16,16,128]{2,1,0:T(8,128)S(1)}, f32[16,16,128]{2,1,0:T(8,128)S(1)}, u32[]{:S(2)}, u32[]{:S(2)}) %collective-permute-start.20) | collective-permute-done | bytes 131104 | tf_op jit(solution)/shard_map/ppermute | solution.py:30
  102.0 0.1 add_add_fusion.1
  102.1 0.1 maximum_multiply_fusion
  102.1 0.1 mul.27
  102.2 0.9 multiply_subtract_fusion
  (32 shorter events, 0.3 us)
Async XLA Ops:
  0.0 13.8 %copy-start = (s32[1,1,1,8]{3,2,1,0:T(1,128)S(1)}, s32[1,1,1,8]{3,2,1,0:T(1,128)}, u32[]{:S(2)}) copy-start(s32[1,1,1,8]{3,2,1,0:T(1,128)} %param.9) | copy-start | bytes 100
  1.2 21.5 %collective-permute-start.3 = (f32[32,32,128]{2,1,0:T(8,128)S(1)}, f32[32,32,128]{2,1,0:T(8,128)S(1)}, u32[]{:S(2)}, u32[]{:S(2)}) collective-permute-start(f32[32,32,128]{2,1,0:T(8,128)S(1)} %bitcast.18), channel_id=1, source_target_pairs={{0,32},{1,33},{2,34},{3,35},{4,36},{5,37},{6,38},{7,39},{8,40},{9,... | collective-permute-start | bytes 1572872 | tf_op jit(solution)/shard_map/ppermute | solution.py:30
  8.4 26.6 %collective-permute-start.2 = (f32[32,32,128]{2,1,0:T(8,128)S(1)}, f32[32,32,128]{2,1,0:T(8,128)S(1)}, u32[]{:S(2)}, u32[]{:S(2)}) collective-permute-start(f32[32,32,128]{2,1,0:T(8,128)S(1)} %bitcast.19), channel_id=1, source_target_pairs={{0,128},{1,129},{2,130},{3,131},{4,132},{5,133},{6,134},{7,135},{8... | collective-permute-start | bytes 1572872 | tf_op jit(solution)/shard_map/ppermute | solution.py:30
  9.7 25.4 %collective-permute-start.1 = (f32[32,32,128]{2,1,0:T(8,128)S(1)}, f32[32,32,128]{2,1,0:T(8,128)S(1)}, u32[]{:S(2)}, u32[]{:S(2)}) collective-permute-start(f32[32,32,128]{2,1,0:T(8,128)S(1)} %bitcast.20), channel_id=1, source_target_pairs={{0,64},{1,65},{2,66},{3,67},{4,68},{5,69},{6,70},{7,71},{8,72},{9,... | collective-permute-start | bytes 1572872 | tf_op jit(solution)/shard_map/ppermute | solution.py:30
  11.8 23.2 %collective-permute-start = (f32[32,32,128]{2,1,0:T(8,128)S(1)}, f32[32,32,128]{2,1,0:T(8,128)S(1)}, u32[]{:S(2)}, u32[]{:S(2)}) collective-permute-start(f32[32,32,128]{2,1,0:T(8,128)S(1)} %bitcast.21), channel_id=1, source_target_pairs={{0,192},{1,193},{2,194},{3,195},{4,196},{5,197},{6,198},{7,199},{8... | collective-permute-start | bytes 1572872 | tf_op jit(solution)/shard_map/ppermute | solution.py:30
  22.6 17.4 %collective-permute-start.7 = (f32[16,32,128]{2,1,0:T(8,128)S(1)}, f32[16,32,128]{2,1,0:T(8,128)S(1)}, u32[]{:S(2)}, u32[]{:S(2)}) collective-permute-start(f32[16,32,128]{2,1,0:T(8,128)S(1)} %get-tuple-element.81), channel_id=1, source_target_pairs={{0,24},{1,25},{2,26},{3,27},{4,28},{5,29},{6,30},{7,31},{8,0},{9,1... | collective-permute-start | bytes 786440 | tf_op jit(solution)/shard_map/ppermute | solution.py:30
  29.7 16.0 %collective-permute-start.6 = (f32[16,32,128]{2,1,0:T(8,128)S(1)}, f32[16,32,128]{2,1,0:T(8,128)S(1)}, u32[]{:S(2)}, u32[]{:S(2)}) collective-permute-start(f32[16,32,128]{2,1,0:T(8,128)S(1)} %get-tuple-element.82), channel_id=1, source_target_pairs={{0,24},{1,25},{2,26},{3,27},{4,28},{5,29},{6,30},{7,31},{8,0},{9,1... | collective-permute-start | bytes 786440 | tf_op jit(solution)/shard_map/ppermute | solution.py:30
  35.1 20.3 %collective-permute-start.5 = (f32[32,32,128]{2,1,0:T(8,128)S(1)}, f32[32,32,128]{2,1,0:T(8,128)S(1)}, u32[]{:S(2)}, u32[]{:S(2)}) collective-permute-start(f32[32,32,128]{2,1,0:T(8,128)S(1)} %collective-permute-done.3.refs_5_), channel_id=1, source_target_pairs={{0,64},{1,65},{2,66},{3,67},{4,68},{5,69},{6,70},{7,71},{8,72},{9,... | collective-permute-start | bytes 1572872 | tf_op jit(solution)/shard_map/ppermute | solution.py:30
  35.4 20.0 %collective-permute-start.4 = (f32[32,32,128]{2,1,0:T(8,128)S(1)}, f32[32,32,128]{2,1,0:T(8,128)S(1)}, u32[]{:S(2)}, u32[]{:S(2)}) collective-permute-start(f32[32,32,128]{2,1,0:T(8,128)S(1)} %collective-permute-done.3.refs_5_), channel_id=1, source_target_pairs={{0,192},{1,193},{2,194},{3,195},{4,196},{5,197},{6,198},{7,199},{8... | collective-permute-start | bytes 1572872 | tf_op jit(solution)/shard_map/ppermute | solution.py:30
  40.1 11.2 %collective-permute-start.9 = (f32[16,32,128]{2,1,0:T(8,128)S(1)}, f32[16,32,128]{2,1,0:T(8,128)S(1)}, u32[]{:S(2)}, u32[]{:S(2)}) collective-permute-start(f32[16,32,128]{2,1,0:T(8,128)S(1)} %collective-permute-done.7), channel_id=1, source_target_pairs={{0,24},{1,25},{2,26},{3,27},{4,28},{5,29},{6,30},{7,31},{8,0},{9,1... | collective-permute-start | bytes 786440 | tf_op jit(solution)/shard_map/ppermute | solution.py:30
  45.7 9.6 %collective-permute-start.8 = (f32[16,32,128]{2,1,0:T(8,128)S(1)}, f32[16,32,128]{2,1,0:T(8,128)S(1)}, u32[]{:S(2)}, u32[]{:S(2)}) collective-permute-start(f32[16,32,128]{2,1,0:T(8,128)S(1)} %collective-permute-done.6), channel_id=1, source_target_pairs={{0,24},{1,25},{2,26},{3,27},{4,28},{5,29},{6,30},{7,31},{8,0},{9,1... | collective-permute-start | bytes 786440 | tf_op jit(solution)/shard_map/ppermute | solution.py:30
  47.4 10.2 %collective-permute-start.15 = (f32[32,32,128]{2,1,0:T(8,128)S(1)}, f32[32,32,128]{2,1,0:T(8,128)S(1)}, u32[]{:S(2)}, u32[]{:S(2)}) collective-permute-start(f32[32,32,128]{2,1,0:T(8,128)S(1)} %bitcast.17), channel_id=1, source_target_pairs={{0,4},{1,5},{2,6},{3,7},{4,0},{5,1},{6,2},{7,3},{8,12},{9,13},{10,... | collective-permute-start | bytes 1572872 | tf_op jit(solution)/shard_map/ppermute | solution.py:30
  51.3 15.9 %collective-permute-start.14 = (f32[32,32,128]{2,1,0:T(8,128)S(1)}, f32[32,32,128]{2,1,0:T(8,128)S(1)}, u32[]{:S(2)}, u32[]{:S(2)}) collective-permute-start(f32[32,32,128]{2,1,0:T(8,128)S(1)} %collective-permute-done.3.refs_5_), channel_id=1, source_target_pairs={{0,128},{1,129},{2,130},{3,131},{4,132},{5,133},{6,134},{7,135},{8... | collective-permute-start | bytes 1572872 | tf_op jit(solution)/shard_map/ppermute | solution.py:30
  55.3 11.9 %collective-permute-start.12 = (f32[32,32,128]{2,1,0:T(8,128)S(1)}, f32[32,32,128]{2,1,0:T(8,128)S(1)}, u32[]{:S(2)}, u32[]{:S(2)}) collective-permute-start(f32[32,32,128]{2,1,0:T(8,128)S(1)} %constant_dynamic-update-slice_fusion.refs_3_), channel_id=1, source_target_pairs={{0,4},{1,5},{2,6},{3,7},{4,0},{5,1},{6,2},{7,3},{8,12},{9,13},{10,... | collective-permute-start | bytes 1572872 | tf_op jit(solution)/shard_map/ppermute | solution.py:30
  55.4 11.8 %collective-permute-start.13 = (f32[32,32,128]{2,1,0:T(8,128)S(1)}, f32[32,32,128]{2,1,0:T(8,128)S(1)}, u32[]{:S(2)}, u32[]{:S(2)}) collective-permute-start(f32[32,32,128]{2,1,0:T(8,128)S(1)} %constant_dynamic-update-slice_fusion.2.refs_4_), channel_id=1, source_target_pairs={{0,4},{1,5},{2,6},{3,7},{4,0},{5,1},{6,2},{7,3},{8,12},{9,13},{10,... | collective-permute-start | bytes 1572872 | tf_op jit(solution)/shard_map/ppermute | solution.py:30
  56.0 17.2 %collective-permute-start.10 = (f32[16,32,128]{2,1,0:T(8,128)S(1)}, f32[16,32,128]{2,1,0:T(8,128)S(1)}, u32[]{:S(2)}, u32[]{:S(2)}) collective-permute-start(f32[16,32,128]{2,1,0:T(8,128)S(1)} %collective-permute-done.8), channel_id=1, source_target_pairs={{0,24},{1,25},{2,26},{3,27},{4,28},{5,29},{6,30},{7,31},{8,0},{9,1... | collective-permute-start | bytes 786440 | tf_op jit(solution)/shard_map/ppermute | solution.py:30
  57.7 15.5 %collective-permute-start.11 = (f32[16,32,128]{2,1,0:T(8,128)S(1)}, f32[16,32,128]{2,1,0:T(8,128)S(1)}, u32[]{:S(2)}, u32[]{:S(2)}) collective-permute-start(f32[16,32,128]{2,1,0:T(8,128)S(1)} %collective-permute-done.9), channel_id=1, source_target_pairs={{0,24},{1,25},{2,26},{3,27},{4,28},{5,29},{6,30},{7,31},{8,0},{9,1... | collective-permute-start | bytes 786440 | tf_op jit(solution)/shard_map/ppermute | solution.py:30
  73.3 2.3 %collective-permute-start.16 = (f32[32,32,128]{2,1,0:T(8,128)S(1)}, f32[32,32,128]{2,1,0:T(8,128)S(1)}, u32[]{:S(2)}, u32[]{:S(2)}) collective-permute-start(f32[32,32,128]{2,1,0:T(8,128)S(1)} %constant_dynamic-update-slice_fusion.4.refs_3_), channel_id=1, source_target_pairs={{0,4},{1,5},{2,6},{3,7},{4,0},{5,1},{6,2},{7,3},{8,12},{9,13},{10,... | collective-permute-start | bytes 1572872 | tf_op jit(solution)/shard_map/ppermute | solution.py:30
  77.7 9.2 %collective-permute-start.21 = (f32[32,16,128]{2,1,0:T(8,128)S(1)}, f32[32,16,128]{2,1,0:T(8,128)S(1)}, u32[]{:S(2)}, u32[]{:S(2)}) collective-permute-start(f32[32,16,128]{2,1,0:T(8,128)S(1)} %get-tuple-element.73), channel_id=1, source_target_pairs={{0,1},{1,2},{2,3},{3,0},{4,5},{5,6},{6,7},{7,4},{8,9},{9,10},{10,1... | collective-permute-start | bytes 786440 | tf_op jit(solution)/shard_map/ppermute | solution.py:30
  79.2 9.8 %collective-permute-start.22 = (f32[32,16,128]{2,1,0:T(8,128)S(1)}, f32[32,16,128]{2,1,0:T(8,128)S(1)}, u32[]{:S(2)}, u32[]{:S(2)}) collective-permute-start(f32[32,16,128]{2,1,0:T(8,128)S(1)} %get-tuple-element.74), channel_id=1, source_target_pairs={{0,3},{1,0},{2,1},{3,2},{4,7},{5,4},{6,5},{7,6},{8,11},{9,8},{10,9... | collective-permute-start | bytes 786440 | tf_op jit(solution)/shard_map/ppermute | solution.py:30
  82.0 10.5 %collective-permute-start.17 = (f32[32,16,128]{2,1,0:T(8,128)S(1)}, f32[32,16,128]{2,1,0:T(8,128)S(1)}, u32[]{:S(2)}, u32[]{:S(2)}) collective-permute-start(f32[32,16,128]{2,1,0:T(8,128)S(1)} %get-tuple-element.64), channel_id=1, source_target_pairs={{0,1},{1,2},{2,3},{3,0},{4,5},{5,6},{6,7},{7,4},{8,9},{9,10},{10,1... | collective-permute-start | bytes 786440 | tf_op jit(solution)/shard_map/ppermute | solution.py:30
  85.1 10.3 %collective-permute-start.18 = (f32[32,16,128]{2,1,0:T(8,128)S(1)}, f32[32,16,128]{2,1,0:T(8,128)S(1)}, u32[]{:S(2)}, u32[]{:S(2)}) collective-permute-start(f32[32,16,128]{2,1,0:T(8,128)S(1)} %get-tuple-element.65), channel_id=1, source_target_pairs={{0,3},{1,0},{2,1},{3,2},{4,7},{5,4},{6,5},{7,6},{8,11},{9,8},{10,9... | collective-permute-start | bytes 786440 | tf_op jit(solution)/shard_map/ppermute | solution.py:30
  89.1 8.6 %collective-permute-start.23 = (f32[16,16,128]{2,1,0:T(8,128)S(1)}, f32[16,16,128]{2,1,0:T(8,128)S(1)}, u32[]{:S(2)}, u32[]{:S(2)}) collective-permute-start(f32[16,16,128]{2,1,0:T(8,128)S(1)} %slice_add_fusion.1), channel_id=1, source_target_pairs={{0,1},{1,2},{2,3},{3,0},{4,5},{5,6},{6,7},{7,4},{8,9},{9,10},{10,1... | collective-permute-start | bytes 393224 | tf_op jit(solution)/shard_map/ppermute | solution.py:30
  89.4 8.2 %collective-permute-start.24 = (f32[16,16,128]{2,1,0:T(8,128)S(1)}, f32[16,16,128]{2,1,0:T(8,128)S(1)}, u32[]{:S(2)}, u32[]{:S(2)}) collective-permute-start(f32[16,16,128]{2,1,0:T(8,128)S(1)} %slice_add_fusion), channel_id=1, source_target_pairs={{0,3},{1,0},{2,1},{3,2},{4,7},{5,4},{6,5},{7,6},{8,11},{9,8},{10,9... | collective-permute-start | bytes 393224 | tf_op jit(solution)/shard_map/ppermute | solution.py:30
  95.4 5.0 %collective-permute-start.19 = (f32[16,16,128]{2,1,0:T(8,128)S(1)}, f32[16,16,128]{2,1,0:T(8,128)S(1)}, u32[]{:S(2)}, u32[]{:S(2)}) collective-permute-start(f32[16,16,128]{2,1,0:T(8,128)S(1)} %slice_add_fusion.3), channel_id=1, source_target_pairs={{0,1},{1,2},{2,3},{3,0},{4,5},{5,6},{6,7},{7,4},{8,9},{9,10},{10,1... | collective-permute-start | bytes 393224 | tf_op jit(solution)/shard_map/ppermute | solution.py:30
  95.7 6.6 %copy-start.1 = (f32[1,1,32,4096]{3,2,1,0:T(8,128)S(1)}, f32[1,1,32,4096]{3,2,1,0:T(8,128)}, u32[]{:S(2)}) copy-start(f32[1,1,32,4096]{3,2,1,0:T(8,128)} %param.7) | copy-start | bytes 1572868
  95.7 6.3 %collective-permute-start.20 = (f32[16,16,128]{2,1,0:T(8,128)S(1)}, f32[16,16,128]{2,1,0:T(8,128)S(1)}, u32[]{:S(2)}, u32[]{:S(2)}) collective-permute-start(f32[16,16,128]{2,1,0:T(8,128)S(1)} %slice_add_fusion.2), channel_id=1, source_target_pairs={{0,3},{1,0},{2,1},{3,2},{4,7},{5,4},{6,5},{7,6},{8,11},{9,8},{10,9... | collective-permute-start | bytes 393224 | tf_op jit(solution)/shard_map/ppermute | solution.py:30

commit v3 on v1

--- a/solution.py
+++ b/solution.py
@@ -12,7 +12,7 @@
 BF16 = jnp.bfloat16
 TILES = 32
 SLOTS = 128
-UNROLL = 32
+UNROLL = 64
 PARTS = ((0, 32), (32, 48), (48, 80), (80, 112), (112, 128))
 
 

time: 103 us -> 103 us (level)
  Pallas kernels: 24.4 us -> 27 us
  starting transfers between devices: 37.9 us -> 36.3 us
    pallas_call x7, Pallas kernels: 24.4 us -> 27 us  [add_sections(): pl.pallas_call(functools.partial(section_kernel, jobs, later, len(lefts),...]
    ppermute x22, starting transfers between devices: 37.9 us -> 36.3 us  [moved(): return lax.ppermute(x, AXES, pairs)]
  transfers between devices with their start and end apart: 22 -> 22, of which waited for: 13 -> 11; matrix products, arithmetic and copies ran while one was open for 2% -> 2% of each run, Pallas kernels for 22% -> 24%
where the time goes in v3:
time: 103 us
  starting transfers between devices  36.3 us (35%)
  waiting for transfers between devices  35.3 us (34%)
  Pallas kernels  27 us (26%)
  local copies, waits for them, and re-layouts  3.11 us (3%)
  other arithmetic  1.17 us (1%)
    ppermute x22, starting transfers between devices, moved(): return lax.ppermute(x, AXES, pairs)  36.3 us
    ppermute x22, waiting for transfers between devices, moved(): return lax.ppermute(x, AXES, pairs)  35.3 us
    pallas_call x7, Pallas kernels, add_sections(): pl.pallas_call(functools.partial(section_kernel, jobs, later, len(lefts),...  27 us
    unnamed x7, local copies, waits for them, and re-layouts  3.01 us
  transfers between devices with their start and end apart: 22, of which 11 were waited for; matrix products, arithmetic and copies ran while one was open for 2% of the time, Pallas kernels for 24%

profile of v3, /device:TPU:30, one launch (start us, length us, event | category | flops | bytes accessed | tf_op | source)
XLA Modules:
  0.0 103.0 jit_solution(4491678045404761440)
XLA Ops:
  0.0 1.1 %copy.7 = f32[4,8,32,128]{3,2,1,0:T(8,128)S(1)} copy(f32[4,8,32,128]{3,1,2,0:T(8,128)} %bitcast.37) | data formatting | bytes 1048576
  1.2 7.3 %collective-permute-start.3 = (f32[32,32,128]{2,1,0:T(8,128)S(1)}, f32[32,32,128]{2,1,0:T(8,128)S(1)}, u32[]{:S(2)}, u32[]{:S(2)}) collective-permute-start(f32[32,32,128]{2,1,0:T(8,128)S(1)} %bitcast.15), channel_id=1, source_target_pairs={{0,32},{1,33},{2,34},{3,35},{4,36},{5,37},{6,38},{7,39},{8,40},{9,... | collective-permute-start | bytes 1572872 | tf_op jit(solution)/shard_map/ppermute | solution.py:30
  8.4 1.2 %collective-permute-start.2 = (f32[32,32,128]{2,1,0:T(8,128)S(1)}, f32[32,32,128]{2,1,0:T(8,128)S(1)}, u32[]{:S(2)}, u32[]{:S(2)}) collective-permute-start(f32[32,32,128]{2,1,0:T(8,128)S(1)} %bitcast.16), channel_id=1, source_target_pairs={{0,128},{1,129},{2,130},{3,131},{4,132},{5,133},{6,134},{7,135},{8... | collective-permute-start | bytes 1572872 | tf_op jit(solution)/shard_map/ppermute | solution.py:30
  9.7 2.2 %collective-permute-start.1 = (f32[32,32,128]{2,1,0:T(8,128)S(1)}, f32[32,32,128]{2,1,0:T(8,128)S(1)}, u32[]{:S(2)}, u32[]{:S(2)}) collective-permute-start(f32[32,32,128]{2,1,0:T(8,128)S(1)} %bitcast.17), channel_id=1, source_target_pairs={{0,64},{1,65},{2,66},{3,67},{4,68},{5,69},{6,70},{7,71},{8,72},{9,... | collective-permute-start | bytes 1572872 | tf_op jit(solution)/shard_map/ppermute | solution.py:30
  11.8 0.0 collective-permute-start
  11.9 0.7 copy.10
  12.6 0.1 pad_add_fusion.refs_0_
  12.6 1.1 %copy.8 = f32[4,8,32,128]{3,2,1,0:T(8,128)S(1)} copy(f32[4,8,32,128]{3,1,2,0:T(8,128)} %bitcast.38) | data formatting | bytes 1048576
  13.8 3.3 %sections_a.1.refs_6_ = f32[129,32,128]{2,1,0:T(8,128)S(1)} custom-call(s32[3]{0:T(128)S(1)} %pad_add_fusion.refs_0_, s32[8,3,64]{2,1,0:T(4,128)S(1)} %bitcast.23, s32[8]{0:T(128)S(1)} %bitcast.30, f32[32,32,128]{2,1,0:T(8,128)S(1)} %bitcast.20, f32[32,32,128]{2,1,0:T(8,128)S(1)} %bitcast.19), custom_call_target="tpu_custom_call" | custom-call | tf_op jit(solution)/shard_map/sections_a/pallas_call | solution.py:182
  17.0 5.6 %collective-permute-done.3.refs_5_ = f32[32,32,128]{2,1,0:T(8,128)S(1)} collective-permute-done((f32[32,32,128]{2,1,0:T(8,128)S(1)}, f32[32,32,128]{2,1,0:T(8,128)S(1)}, u32[]{:S(2)}, u32[]{:S(2)}) %collective-permute-start.3) | collective-permute-done | bytes 524320 | tf_op jit(solution)/shard_map/ppermute | solution.py:30
  22.6 7.0 %collective-permute-start.6 = (f32[32,32,128]{2,1,0:T(8,128)S(1)}, f32[32,32,128]{2,1,0:T(8,128)S(1)}, u32[]{:S(2)}, u32[]{:S(2)}) collective-permute-start(f32[32,32,128]{2,1,0:T(8,128)S(1)} %bitcast.21), channel_id=1, source_target_pairs={{0,24},{1,25},{2,26},{3,27},{4,28},{5,29},{6,30},{7,31},{8,0},{9,1... | collective-permute-start | bytes 1572872 | tf_op jit(solution)/shard_map/ppermute | solution.py:30
  29.6 0.0 collective-permute-done.2.refs_8_
  29.6 2.5 %collective-permute-done.1.refs_5_ = f32[32,32,128]{2,1,0:T(8,128)S(1)} collective-permute-done((f32[32,32,128]{2,1,0:T(8,128)S(1)}, f32[32,32,128]{2,1,0:T(8,128)S(1)}, u32[]{:S(2)}, u32[]{:S(2)}) %collective-permute-start.1) | collective-permute-done | bytes 524320 | tf_op jit(solution)/shard_map/ppermute | solution.py:30
  32.1 2.4 %collective-permute-done.refs_4_ = f32[32,32,128]{2,1,0:T(8,128)S(1)} collective-permute-done((f32[32,32,128]{2,1,0:T(8,128)S(1)}, f32[32,32,128]{2,1,0:T(8,128)S(1)}, u32[]{:S(2)}, u32[]{:S(2)}) %collective-permute-start) | collective-permute-done | bytes 524320 | tf_op jit(solution)/shard_map/ppermute | solution.py:30
  34.6 0.6 collective-permute-start.5
  35.2 1.4 %collective-permute-start.4 = (f32[32,32,128]{2,1,0:T(8,128)S(1)}, f32[32,32,128]{2,1,0:T(8,128)S(1)}, u32[]{:S(2)}, u32[]{:S(2)}) collective-permute-start(f32[32,32,128]{2,1,0:T(8,128)S(1)} %collective-permute-done.3.refs_5_), channel_id=1, source_target_pairs={{0,192},{1,193},{2,194},{3,195},{4,196},{5,197},{6,198},{7,199},{8... | collective-permute-start | bytes 1572872 | tf_op jit(solution)/shard_map/ppermute | solution.py:30
  36.6 7.4 %collective-permute-done.6.refs_3_ = f32[32,32,128]{2,1,0:T(8,128)S(1)} collective-permute-done((f32[32,32,128]{2,1,0:T(8,128)S(1)}, f32[32,32,128]{2,1,0:T(8,128)S(1)}, u32[]{:S(2)}, u32[]{:S(2)}) %collective-permute-start.6) | collective-permute-done | bytes 524320 | tf_op jit(solution)/shard_map/ppermute | solution.py:30
  44.0 1.8 %collective-permute-start.7 = (f32[32,32,128]{2,1,0:T(8,128)S(1)}, f32[32,32,128]{2,1,0:T(8,128)S(1)}, u32[]{:S(2)}, u32[]{:S(2)}) collective-permute-start(f32[32,32,128]{2,1,0:T(8,128)S(1)} %collective-permute-done.6.refs_3_), channel_id=1, source_target_pairs={{0,24},{1,25},{2,26},{3,27},{4,28},{5,29},{6,30},{7,31},{8,0},{9,1... | collective-permute-start | bytes 1572872 | tf_op jit(solution)/shard_map/ppermute | solution.py:30
  45.8 1.2 %collective-permute-start.11 = (f32[32,32,128]{2,1,0:T(8,128)S(1)}, f32[32,32,128]{2,1,0:T(8,128)S(1)}, u32[]{:S(2)}, u32[]{:S(2)}) collective-permute-start(f32[32,32,128]{2,1,0:T(8,128)S(1)} %collective-permute-done.3.refs_5_), channel_id=1, source_target_pairs={{0,128},{1,129},{2,130},{3,131},{4,132},{5,133},{6,134},{7,135},{8... | collective-permute-start | bytes 1572872 | tf_op jit(solution)/shard_map/ppermute | solution.py:30
  47.0 4.1 %sections_b.1 = (f32[129,32,128]{2,1,0:T(8,128)S(1)}, bf16[32,128,128]{2,1,0:T(8,128)(2,1)S(1)}) custom-call(s32[3]{0:T(128)S(1)} %pad_add_fusion.refs_0_, s32[8,3,64]{2,1,0:T(4,128)S(1)} %bitcast.24, s32[8]{0:T(128)S(1)} %bitcast.31, f32[32,32,128]{2,1,0:T(8,128)S(1)} %collective-permute-done.6.refs_3_, f32[32,32,128]{2,1,0:T(8,128)S(1)} %collective-permute-done.refs_4_, ...), custom_call_target="tpu_custom_call" | custom-call | tf_op jit(solution)/shard_map/sections_b/pallas_call | solution.py:182
  51.1 0.3 collective-permute-start.9
  51.4 5.1 %collective-permute-done.7.refs_4_ = f32[32,32,128]{2,1,0:T(8,128)S(1)} collective-permute-done((f32[32,32,128]{2,1,0:T(8,128)S(1)}, f32[32,32,128]{2,1,0:T(8,128)S(1)}, u32[]{:S(2)}, u32[]{:S(2)}) %collective-permute-start.7) | collective-permute-done | bytes 524320 | tf_op jit(solution)/shard_map/ppermute | solution.py:30
  56.6 4.3 %collective-permute-start.8 = (f32[32,32,128]{2,1,0:T(8,128)S(1)}, f32[32,32,128]{2,1,0:T(8,128)S(1)}, u32[]{:S(2)}, u32[]{:S(2)}) collective-permute-start(f32[32,32,128]{2,1,0:T(8,128)S(1)} %collective-permute-done.7.refs_4_), channel_id=1, source_target_pairs={{0,24},{1,25},{2,26},{3,27},{4,28},{5,29},{6,30},{7,31},{8,0},{9,1... | collective-permute-start | bytes 1572872 | tf_op jit(solution)/shard_map/ppermute | solution.py:30
  60.9 5.7 %sections_c.1.refs_9_ = f32[129,32,128]{2,1,0:T(8,128)S(1)} custom-call(s32[3]{0:T(128)S(1)} %pad_add_fusion.refs_0_, s32[8,3,64]{2,1,0:T(4,128)S(1)} %bitcast.25, s32[8]{0:T(128)S(1)} %bitcast.32, f32[32,32,128]{2,1,0:T(8,128)S(1)} %collective-permute-done.12.refs_3_, f32[32,32,128]{2,1,0:T(8,128)S(1)} %collective-permute-done.7.refs_4_, ...), custom_call_target="tpu_custom_call" | custom-call | tf_op jit(solution)/shard_map/sections_c/pallas_call | solution.py:182
  66.6 6.6 %sections_d.1 = (f32[129,32,128]{2,1,0:T(8,128)S(1)}, bf16[32,128,128]{2,1,0:T(8,128)(2,1)S(1)}) custom-call(s32[3]{0:T(128)S(1)} %pad_add_fusion.refs_0_, s32[8,3,64]{2,1,0:T(4,128)S(1)} %bitcast.26, s32[8]{0:T(128)S(1)} %bitcast.33, f32[32,32,128]{2,1,0:T(8,128)S(1)} %collective-permute-done.9.refs_3_, f32[32,32,128]{2,1,0:T(8,128)S(1)} %collective-permute-done.10.refs_4_, ...), custom_call_target="tpu_custom_call" | custom-call | tf_op jit(solution)/shard_map/sections_d/pallas_call | solution.py:182
  73.2 0.3 collective-permute-start.13
  73.5 2.5 %sections_e.1.refs_5_ = f32[129,32,128]{2,1,0:T(8,128)S(1)} custom-call(s32[3]{0:T(128)S(1)} %pad_add_fusion.refs_0_, s32[8,3,64]{2,1,0:T(4,128)S(1)} %bitcast.27, s32[8]{0:T(128)S(1)} %bitcast.34, f32[32,32,128]{2,1,0:T(8,128)S(1)} %collective-permute-done.8.refs_3_, bf16[32,128,128]{2,1,0:T(8,128)(2,1)S(1)} %get-tuple-element.57.refs_4_, ...), custom_call_target="tpu_custom_call" | custom-call | tf_op jit(solution)/shard_map/sections_e/pallas_call | solution.py:182
  76.0 2.4 %sections_f1.1 = (f32[32,16,128]{2,1,0:T(8,128)S(1)}, f32[16,16,128]{2,1,0:T(8,128)S(1)}, f32[32,16,128]{2,1,0:T(8,128)S(1)}, f32[32,16,128]{2,1,0:T(8,128)S(1)}, f32[16,16,128]{2,1,0:T(8,128)S(1)}) custom-call(s32[3]{0:T(128)S(1)} %pad_add_fusion.refs_0_, s32[8,3,64]{2,1,0:T(4,128)S(1)} %bitcast.28, s32[8]{0:T(128)S(1)} %bitcast.35, ...), custom_call_target="tpu_custom_call" | custom-call | tf_op jit(solution)/shard_map/sections_f1/pallas_call | solution.py:182
  78.5 0.7 collective-permute-start.18
  79.2 1.4 %collective-permute-start.19 = (f32[32,16,128]{2,1,0:T(8,128)S(1)}, f32[32,16,128]{2,1,0:T(8,128)S(1)}, u32[]{:S(2)}, u32[]{:S(2)}) collective-permute-start(f32[32,16,128]{2,1,0:T(8,128)S(1)} %get-tuple-element.70), channel_id=1, source_target_pairs={{0,3},{1,0},{2,1},{3,2},{4,7},{5,4},{6,5},{7,6},{8,11},{9,8},{10,9... | collective-permute-start | bytes 786440 | tf_op jit(solution)/shard_map/ppermute | solution.py:30
  80.6 2.4 %sections_f0.1 = (f32[32,16,128]{2,1,0:T(8,128)S(1)}, f32[16,16,128]{2,1,0:T(8,128)S(1)}, f32[32,16,128]{2,1,0:T(8,128)S(1)}, f32[32,16,128]{2,1,0:T(8,128)S(1)}, f32[16,16,128]{2,1,0:T(8,128)S(1)}) custom-call(s32[3]{0:T(128)S(1)} %pad_add_fusion.refs_0_, s32[8,3,64]{2,1,0:T(4,128)S(1)} %bitcast.29, s32[8]{0:T(128)S(1)} %bitcast.36, ...), custom_call_target="tpu_custom_call" | custom-call | tf_op jit(solution)/shard_map/sections_f0/pallas_call | solution.py:182
  83.0 1.9 %collective-permute-start.14 = (f32[32,16,128]{2,1,0:T(8,128)S(1)}, f32[32,16,128]{2,1,0:T(8,128)S(1)}, u32[]{:S(2)}, u32[]{:S(2)}) collective-permute-start(f32[32,16,128]{2,1,0:T(8,128)S(1)} %get-tuple-element.60), channel_id=1, source_target_pairs={{0,1},{1,2},{2,3},{3,0},{4,5},{5,6},{6,7},{7,4},{8,9},{9,10},{10,1... | collective-permute-start | bytes 786440 | tf_op jit(solution)/shard_map/ppermute | solution.py:30
  84.9 0.2 collective-permute-start.15
  85.1 2.6 %collective-permute-done.18 = f32[32,16,128]{2,1,0:T(8,128)S(1)} collective-permute-done((f32[32,16,128]{2,1,0:T(8,128)S(1)}, f32[32,16,128]{2,1,0:T(8,128)S(1)}, u32[]{:S(2)}, u32[]{:S(2)}) %collective-permute-start.18) | collective-permute-done | bytes 262176 | tf_op jit(solution)/shard_map/ppermute | solution.py:30
  87.7 1.2 %collective-permute-done.19 = f32[32,16,128]{2,1,0:T(8,128)S(1)} collective-permute-done((f32[32,16,128]{2,1,0:T(8,128)S(1)}, f32[32,16,128]{2,1,0:T(8,128)S(1)}, u32[]{:S(2)}, u32[]{:S(2)}) %collective-permute-start.19) | collective-permute-done | bytes 262176 | tf_op jit(solution)/shard_map/ppermute | solution.py:30
  88.9 1.0 collective-permute-start.20
  89.9 1.2 %collective-permute-start.21 = (f32[16,16,128]{2,1,0:T(8,128)S(1)}, f32[16,16,128]{2,1,0:T(8,128)S(1)}, u32[]{:S(2)}, u32[]{:S(2)}) collective-permute-start(f32[16,16,128]{2,1,0:T(8,128)S(1)} %slice_add_fusion), channel_id=1, source_target_pairs={{0,3},{1,0},{2,1},{3,2},{4,7},{5,4},{6,5},{7,6},{8,11},{9,8},{10,9... | collective-permute-start | bytes 393224 | tf_op jit(solution)/shard_map/ppermute | solution.py:30
  91.1 2.2 %collective-permute-done.14 = f32[32,16,128]{2,1,0:T(8,128)S(1)} collective-permute-done((f32[32,16,128]{2,1,0:T(8,128)S(1)}, f32[32,16,128]{2,1,0:T(8,128)S(1)}, u32[]{:S(2)}, u32[]{:S(2)}) %collective-permute-start.14) | collective-permute-done | bytes 262176 | tf_op jit(solution)/shard_map/ppermute | solution.py:30
  93.3 2.1 %collective-permute-done.15 = f32[32,16,128]{2,1,0:T(8,128)S(1)} collective-permute-done((f32[32,16,128]{2,1,0:T(8,128)S(1)}, f32[32,16,128]{2,1,0:T(8,128)S(1)}, u32[]{:S(2)}, u32[]{:S(2)}) %collective-permute-start.15) | collective-permute-done | bytes 262176 | tf_op jit(solution)/shard_map/ppermute | solution.py:30
  95.4 0.1 collective-permute-start.16
  95.5 0.0 copy-start.1
  95.6 2.0 %collective-permute-start.17 = (f32[16,16,128]{2,1,0:T(8,128)S(1)}, f32[16,16,128]{2,1,0:T(8,128)S(1)}, u32[]{:S(2)}, u32[]{:S(2)}) collective-permute-start(f32[16,16,128]{2,1,0:T(8,128)S(1)} %slice_add_fusion.2), channel_id=1, source_target_pairs={{0,3},{1,0},{2,1},{3,2},{4,7},{5,4},{6,5},{7,6},{8,11},{9,8},{10,9... | collective-permute-start | bytes 393224 | tf_op jit(solution)/shard_map/ppermute | solution.py:30
  97.6 2.8 %collective-permute-done.16 = f32[16,16,128]{2,1,0:T(8,128)S(1)} collective-permute-done((f32[16,16,128]{2,1,0:T(8,128)S(1)}, f32[16,16,128]{2,1,0:T(8,128)S(1)}, u32[]{:S(2)}, u32[]{:S(2)}) %collective-permute-start.16) | collective-permute-done | bytes 131104 | tf_op jit(solution)/shard_map/ppermute | solution.py:30
  100.4 1.4 %collective-permute-done.17 = f32[16,16,128]{2,1,0:T(8,128)S(1)} collective-permute-done((f32[16,16,128]{2,1,0:T(8,128)S(1)}, f32[16,16,128]{2,1,0:T(8,128)S(1)}, u32[]{:S(2)}, u32[]{:S(2)}) %collective-permute-start.17) | collective-permute-done | bytes 131104 | tf_op jit(solution)/shard_map/ppermute | solution.py:30
  101.8 0.1 add_add_fusion.1
  101.9 0.1 maximum_multiply_fusion
  102.0 0.1 mul.27
  102.1 0.8 multiply_subtract_fusion
  (19 shorter events, 0.1 us)
Async XLA Ops:
  0.0 13.8 %copy-start = (s32[1,1,1,8]{3,2,1,0:T(1,128)S(1)}, s32[1,1,1,8]{3,2,1,0:T(1,128)}, u32[]{:S(2)}) copy-start(s32[1,1,1,8]{3,2,1,0:T(1,128)} %param.9) | copy-start | bytes 100
  1.2 21.5 %collective-permute-start.3 = (f32[32,32,128]{2,1,0:T(8,128)S(1)}, f32[32,32,128]{2,1,0:T(8,128)S(1)}, u32[]{:S(2)}, u32[]{:S(2)}) collective-permute-start(f32[32,32,128]{2,1,0:T(8,128)S(1)} %bitcast.15), channel_id=1, source_target_pairs={{0,32},{1,33},{2,34},{3,35},{4,36},{5,37},{6,38},{7,39},{8,40},{9,... | collective-permute-start | bytes 1572872 | tf_op jit(solution)/shard_map/ppermute | solution.py:30
  8.4 21.2 %collective-permute-start.2 = (f32[32,32,128]{2,1,0:T(8,128)S(1)}, f32[32,32,128]{2,1,0:T(8,128)S(1)}, u32[]{:S(2)}, u32[]{:S(2)}) collective-permute-start(f32[32,32,128]{2,1,0:T(8,128)S(1)} %bitcast.16), channel_id=1, source_target_pairs={{0,128},{1,129},{2,130},{3,131},{4,132},{5,133},{6,134},{7,135},{8... | collective-permute-start | bytes 1572872 | tf_op jit(solution)/shard_map/ppermute | solution.py:30
  9.7 22.5 %collective-permute-start.1 = (f32[32,32,128]{2,1,0:T(8,128)S(1)}, f32[32,32,128]{2,1,0:T(8,128)S(1)}, u32[]{:S(2)}, u32[]{:S(2)}) collective-permute-start(f32[32,32,128]{2,1,0:T(8,128)S(1)} %bitcast.17), channel_id=1, source_target_pairs={{0,64},{1,65},{2,66},{3,67},{4,68},{5,69},{6,70},{7,71},{8,72},{9,... | collective-permute-start | bytes 1572872 | tf_op jit(solution)/shard_map/ppermute | solution.py:30
  11.8 22.7 %collective-permute-start = (f32[32,32,128]{2,1,0:T(8,128)S(1)}, f32[32,32,128]{2,1,0:T(8,128)S(1)}, u32[]{:S(2)}, u32[]{:S(2)}) collective-permute-start(f32[32,32,128]{2,1,0:T(8,128)S(1)} %bitcast.18), channel_id=1, source_target_pairs={{0,192},{1,193},{2,194},{3,195},{4,196},{5,197},{6,198},{7,199},{8... | collective-permute-start | bytes 1572872 | tf_op jit(solution)/shard_map/ppermute | solution.py:30
  22.6 21.4 %collective-permute-start.6 = (f32[32,32,128]{2,1,0:T(8,128)S(1)}, f32[32,32,128]{2,1,0:T(8,128)S(1)}, u32[]{:S(2)}, u32[]{:S(2)}) collective-permute-start(f32[32,32,128]{2,1,0:T(8,128)S(1)} %bitcast.21), channel_id=1, source_target_pairs={{0,24},{1,25},{2,26},{3,27},{4,28},{5,29},{6,30},{7,31},{8,0},{9,1... | collective-permute-start | bytes 1572872 | tf_op jit(solution)/shard_map/ppermute | solution.py:30
  34.6 16.6 %collective-permute-start.5 = (f32[32,32,128]{2,1,0:T(8,128)S(1)}, f32[32,32,128]{2,1,0:T(8,128)S(1)}, u32[]{:S(2)}, u32[]{:S(2)}) collective-permute-start(f32[32,32,128]{2,1,0:T(8,128)S(1)} %collective-permute-done.3.refs_5_), channel_id=1, source_target_pairs={{0,64},{1,65},{2,66},{3,67},{4,68},{5,69},{6,70},{7,71},{8,72},{9,... | collective-permute-start | bytes 1572872 | tf_op jit(solution)/shard_map/ppermute | solution.py:30
  35.2 16.3 %collective-permute-start.4 = (f32[32,32,128]{2,1,0:T(8,128)S(1)}, f32[32,32,128]{2,1,0:T(8,128)S(1)}, u32[]{:S(2)}, u32[]{:S(2)}) collective-permute-start(f32[32,32,128]{2,1,0:T(8,128)S(1)} %collective-permute-done.3.refs_5_), channel_id=1, source_target_pairs={{0,192},{1,193},{2,194},{3,195},{4,196},{5,197},{6,198},{7,199},{8... | collective-permute-start | bytes 1572872 | tf_op jit(solution)/shard_map/ppermute | solution.py:30
  44.0 12.6 %collective-permute-start.7 = (f32[32,32,128]{2,1,0:T(8,128)S(1)}, f32[32,32,128]{2,1,0:T(8,128)S(1)}, u32[]{:S(2)}, u32[]{:S(2)}) collective-permute-start(f32[32,32,128]{2,1,0:T(8,128)S(1)} %collective-permute-done.6.refs_3_), channel_id=1, source_target_pairs={{0,24},{1,25},{2,26},{3,27},{4,28},{5,29},{6,30},{7,31},{8,0},{9,1... | collective-permute-start | bytes 1572872 | tf_op jit(solution)/shard_map/ppermute | solution.py:30
  45.8 15.1 %collective-permute-start.12 = (f32[32,32,128]{2,1,0:T(8,128)S(1)}, f32[32,32,128]{2,1,0:T(8,128)S(1)}, u32[]{:S(2)}, u32[]{:S(2)}) collective-permute-start(f32[32,32,128]{2,1,0:T(8,128)S(1)} %bitcast.22), channel_id=1, source_target_pairs={{0,4},{1,5},{2,6},{3,7},{4,0},{5,1},{6,2},{7,3},{8,12},{9,13},{10,... | collective-permute-start | bytes 1572872 | tf_op jit(solution)/shard_map/ppermute | solution.py:30
  45.8 20.8 %collective-permute-start.11 = (f32[32,32,128]{2,1,0:T(8,128)S(1)}, f32[32,32,128]{2,1,0:T(8,128)S(1)}, u32[]{:S(2)}, u32[]{:S(2)}) collective-permute-start(f32[32,32,128]{2,1,0:T(8,128)S(1)} %collective-permute-done.3.refs_5_), channel_id=1, source_target_pairs={{0,128},{1,129},{2,130},{3,131},{4,132},{5,133},{6,134},{7,135},{8... | collective-permute-start | bytes 1572872 | tf_op jit(solution)/shard_map/ppermute | solution.py:30
  51.1 15.4 %collective-permute-start.9 = (f32[32,32,128]{2,1,0:T(8,128)S(1)}, f32[32,32,128]{2,1,0:T(8,128)S(1)}, u32[]{:S(2)}, u32[]{:S(2)}) collective-permute-start(f32[32,32,128]{2,1,0:T(8,128)S(1)} %collective-permute-done.6.refs_3_), channel_id=1, source_target_pairs={{0,4},{1,5},{2,6},{3,7},{4,0},{5,1},{6,2},{7,3},{8,12},{9,13},{10,... | collective-permute-start | bytes 1572872 | tf_op jit(solution)/shard_map/ppermute | solution.py:30
  56.6 10.0 %collective-permute-start.10 = (f32[32,32,128]{2,1,0:T(8,128)S(1)}, f32[32,32,128]{2,1,0:T(8,128)S(1)}, u32[]{:S(2)}, u32[]{:S(2)}) collective-permute-start(f32[32,32,128]{2,1,0:T(8,128)S(1)} %collective-permute-done.7.refs_4_), channel_id=1, source_target_pairs={{0,4},{1,5},{2,6},{3,7},{4,0},{5,1},{6,2},{7,3},{8,12},{9,13},{10,... | collective-permute-start | bytes 1572872 | tf_op jit(solution)/shard_map/ppermute | solution.py:30
  56.6 16.6 %collective-permute-start.8 = (f32[32,32,128]{2,1,0:T(8,128)S(1)}, f32[32,32,128]{2,1,0:T(8,128)S(1)}, u32[]{:S(2)}, u32[]{:S(2)}) collective-permute-start(f32[32,32,128]{2,1,0:T(8,128)S(1)} %collective-permute-done.7.refs_4_), channel_id=1, source_target_pairs={{0,24},{1,25},{2,26},{3,27},{4,28},{5,29},{6,30},{7,31},{8,0},{9,1... | collective-permute-start | bytes 1572872 | tf_op jit(solution)/shard_map/ppermute | solution.py:30
  73.2 2.8 %collective-permute-start.13 = (f32[32,32,128]{2,1,0:T(8,128)S(1)}, f32[32,32,128]{2,1,0:T(8,128)S(1)}, u32[]{:S(2)}, u32[]{:S(2)}) collective-permute-start(f32[32,32,128]{2,1,0:T(8,128)S(1)} %collective-permute-done.8.refs_3_), channel_id=1, source_target_pairs={{0,4},{1,5},{2,6},{3,7},{4,0},{5,1},{6,2},{7,3},{8,12},{9,13},{10,... | collective-permute-start | bytes 1572872 | tf_op jit(solution)/shard_map/ppermute | solution.py:30
  78.5 9.2 %collective-permute-start.18 = (f32[32,16,128]{2,1,0:T(8,128)S(1)}, f32[32,16,128]{2,1,0:T(8,128)S(1)}, u32[]{:S(2)}, u32[]{:S(2)}) collective-permute-start(f32[32,16,128]{2,1,0:T(8,128)S(1)} %get-tuple-element.69), channel_id=1, source_target_pairs={{0,1},{1,2},{2,3},{3,0},{4,5},{5,6},{6,7},{7,4},{8,9},{9,10},{10,1... | collective-permute-start | bytes 786440 | tf_op jit(solution)/shard_map/ppermute | solution.py:30
  79.2 9.7 %collective-permute-start.19 = (f32[32,16,128]{2,1,0:T(8,128)S(1)}, f32[32,16,128]{2,1,0:T(8,128)S(1)}, u32[]{:S(2)}, u32[]{:S(2)}) collective-permute-start(f32[32,16,128]{2,1,0:T(8,128)S(1)} %get-tuple-element.70), channel_id=1, source_target_pairs={{0,3},{1,0},{2,1},{3,2},{4,7},{5,4},{6,5},{7,6},{8,11},{9,8},{10,9... | collective-permute-start | bytes 786440 | tf_op jit(solution)/shard_map/ppermute | solution.py:30
  83.0 10.3 %collective-permute-start.14 = (f32[32,16,128]{2,1,0:T(8,128)S(1)}, f32[32,16,128]{2,1,0:T(8,128)S(1)}, u32[]{:S(2)}, u32[]{:S(2)}) collective-permute-start(f32[32,16,128]{2,1,0:T(8,128)S(1)} %get-tuple-element.60), channel_id=1, source_target_pairs={{0,1},{1,2},{2,3},{3,0},{4,5},{5,6},{6,7},{7,4},{8,9},{9,10},{10,1... | collective-permute-start | bytes 786440 | tf_op jit(solution)/shard_map/ppermute | solution.py:30
  84.9 10.5 %collective-permute-start.15 = (f32[32,16,128]{2,1,0:T(8,128)S(1)}, f32[32,16,128]{2,1,0:T(8,128)S(1)}, u32[]{:S(2)}, u32[]{:S(2)}) collective-permute-start(f32[32,16,128]{2,1,0:T(8,128)S(1)} %get-tuple-element.61), channel_id=1, source_target_pairs={{0,3},{1,0},{2,1},{3,2},{4,7},{5,4},{6,5},{7,6},{8,11},{9,8},{10,9... | collective-permute-start | bytes 786440 | tf_op jit(solution)/shard_map/ppermute | solution.py:30
  88.9 8.7 %collective-permute-start.20 = (f32[16,16,128]{2,1,0:T(8,128)S(1)}, f32[16,16,128]{2,1,0:T(8,128)S(1)}, u32[]{:S(2)}, u32[]{:S(2)}) collective-permute-start(f32[16,16,128]{2,1,0:T(8,128)S(1)} %slice_add_fusion.1), channel_id=1, source_target_pairs={{0,1},{1,2},{2,3},{3,0},{4,5},{5,6},{6,7},{7,4},{8,9},{9,10},{10,1... | collective-permute-start | bytes 393224 | tf_op jit(solution)/shard_map/ppermute | solution.py:30
  89.9 7.7 %collective-permute-start.21 = (f32[16,16,128]{2,1,0:T(8,128)S(1)}, f32[16,16,128]{2,1,0:T(8,128)S(1)}, u32[]{:S(2)}, u32[]{:S(2)}) collective-permute-start(f32[16,16,128]{2,1,0:T(8,128)S(1)} %slice_add_fusion), channel_id=1, source_target_pairs={{0,3},{1,0},{2,1},{3,2},{4,7},{5,4},{6,5},{7,6},{8,11},{9,8},{10,9... | collective-permute-start | bytes 393224 | tf_op jit(solution)/shard_map/ppermute | solution.py:30
  95.4 5.0 %collective-permute-start.16 = (f32[16,16,128]{2,1,0:T(8,128)S(1)}, f32[16,16,128]{2,1,0:T(8,128)S(1)}, u32[]{:S(2)}, u32[]{:S(2)}) collective-permute-start(f32[16,16,128]{2,1,0:T(8,128)S(1)} %slice_add_fusion.3), channel_id=1, source_target_pairs={{0,1},{1,2},{2,3},{3,0},{4,5},{5,6},{6,7},{7,4},{8,9},{9,10},{10,1... | collective-permute-start | bytes 393224 | tf_op jit(solution)/shard_map/ppermute | solution.py:30
  95.5 6.6 %copy-start.1 = (f32[1,1,32,4096]{3,2,1,0:T(8,128)S(1)}, f32[1,1,32,4096]{3,2,1,0:T(8,128)}, u32[]{:S(2)}) copy-start(f32[1,1,32,4096]{3,2,1,0:T(8,128)} %param.7) | copy-start | bytes 1572868
  95.6 6.3 %collective-permute-start.17 = (f32[16,16,128]{2,1,0:T(8,128)S(1)}, f32[16,16,128]{2,1,0:T(8,128)S(1)}, u32[]{:S(2)}, u32[]{:S(2)}) collective-permute-start(f32[16,16,128]{2,1,0:T(8,128)S(1)} %slice_add_fusion.2), channel_id=1, source_target_pairs={{0,3},{1,0},{2,1},{3,2},{4,7},{5,4},{6,5},{7,6},{8,11},{9,8},{10,9... | collective-permute-start | bytes 393224 | tf_op jit(solution)/shard_map/ppermute | solution.py:30

commit v4 on v3

--- a/solution.py
+++ b/solution.py
@@ -92,7 +92,7 @@
         k, _, _, choices = job
 
         def interleave(ref):
-            @pl.loop(0, TILES, unroll=4)
+            @pl.loop(0, TILES, unroll=8)
             def _(t):
                 r = ref[t]
                 rr = pltpu.roll(r, 64, 1)
@@ -106,7 +106,7 @@
             for offset, index in choices:
                 pl.when(want == offset)(functools.partial(interleave, rights[index]))
 
-        @pl.loop(0, TILES, unroll=4)
+        @pl.loop(0, TILES, unroll=8)
         def _(t):
             h, low = split(rows[t])
             target[t, 0:64] = h.astype(BF16)
@@ -121,7 +121,7 @@
     def split_panels(j):
         left = lefts[jobs[j][2]]
 
-        @pl.loop(0, TILES, unroll=4)
+        @pl.loop(0, TILES, unroll=8)
         def _(t):
             split_left(left, t)
             if made:

time: 103 us -> 102 us (level)
  Pallas kernels: 27 us -> 21.9 us
  waiting for transfers between devices: 35.3 us -> 39.2 us
    pallas_call x7, Pallas kernels: 27 us -> 21.9 us  [add_sections(): pl.pallas_call(functools.partial(section_kernel, jobs, later, len(lefts),...]
    ppermute x22, waiting for transfers between devices: 35.3 us -> 39.2 us  [moved(): return lax.ppermute(x, AXES, pairs)]
  transfers between devices with their start and end apart: 22 -> 22, of which waited for: 11 -> 12; matrix products, arithmetic and copies ran while one was open for 2% -> 2% of each run, Pallas kernels for 24% -> 20%
where the time goes in v4:
time: 102 us; the launch traced here: 101 us
  waiting for transfers between devices  39.2 us (38%)
  starting transfers between devices  35.9 us (35%)
  Pallas kernels  21.9 us (21%)
  local copies, waits for them, and re-layouts  3.11 us (3%)
  other arithmetic  1.17 us (1%)
    ppermute x22, waiting for transfers between devices, moved(): return lax.ppermute(x, AXES, pairs)  39.2 us
    ppermute x22, starting transfers between devices, moved(): return lax.ppermute(x, AXES, pairs)  35.9 us
    pallas_call x7, Pallas kernels, add_sections(): pl.pallas_call(functools.partial(section_kernel, jobs, later, len(lefts),...  21.9 us
    unnamed x7, local copies, waits for them, and re-layouts  3.01 us
  transfers between devices with their start and end apart: 22, of which 12 were waited for; matrix products, arithmetic and copies ran while one was open for 2% of the time, Pallas kernels for 20%

profile of v4, /device:TPU:30, one launch (start us, length us, event | category | flops | bytes accessed | tf_op | source)
XLA Modules:
  0.0 101.5 jit_solution(11926633195214558)
XLA Ops:
  0.0 1.1 %copy.7 = f32[4,8,32,128]{3,2,1,0:T(8,128)S(1)} copy(f32[4,8,32,128]{3,1,2,0:T(8,128)} %bitcast.37) | data formatting | bytes 1048576
  1.2 7.3 %collective-permute-start.3 = (f32[32,32,128]{2,1,0:T(8,128)S(1)}, f32[32,32,128]{2,1,0:T(8,128)S(1)}, u32[]{:S(2)}, u32[]{:S(2)}) collective-permute-start(f32[32,32,128]{2,1,0:T(8,128)S(1)} %bitcast.15), channel_id=1, source_target_pairs={{0,32},{1,33},{2,34},{3,35},{4,36},{5,37},{6,38},{7,39},{8,40},{9,... | collective-permute-start | bytes 1572872 | tf_op jit(solution)/shard_map/ppermute | solution.py:30
  8.4 1.2 %collective-permute-start.2 = (f32[32,32,128]{2,1,0:T(8,128)S(1)}, f32[32,32,128]{2,1,0:T(8,128)S(1)}, u32[]{:S(2)}, u32[]{:S(2)}) collective-permute-start(f32[32,32,128]{2,1,0:T(8,128)S(1)} %bitcast.16), channel_id=1, source_target_pairs={{0,128},{1,129},{2,130},{3,131},{4,132},{5,133},{6,134},{7,135},{8... | collective-permute-start | bytes 1572872 | tf_op jit(solution)/shard_map/ppermute | solution.py:30
  9.7 2.2 %collective-permute-start.1 = (f32[32,32,128]{2,1,0:T(8,128)S(1)}, f32[32,32,128]{2,1,0:T(8,128)S(1)}, u32[]{:S(2)}, u32[]{:S(2)}) collective-permute-start(f32[32,32,128]{2,1,0:T(8,128)S(1)} %bitcast.17), channel_id=1, source_target_pairs={{0,64},{1,65},{2,66},{3,67},{4,68},{5,69},{6,70},{7,71},{8,72},{9,... | collective-permute-start | bytes 1572872 | tf_op jit(solution)/shard_map/ppermute | solution.py:30
  11.9 0.7 copy.10
  12.6 0.1 pad_add_fusion.refs_0_
  12.6 1.1 %copy.8 = f32[4,8,32,128]{3,2,1,0:T(8,128)S(1)} copy(f32[4,8,32,128]{3,1,2,0:T(8,128)} %bitcast.38) | data formatting | bytes 1048576
  13.8 2.7 %sections_a.1.refs_6_ = f32[129,32,128]{2,1,0:T(8,128)S(1)} custom-call(s32[3]{0:T(128)S(1)} %pad_add_fusion.refs_0_, s32[8,3,64]{2,1,0:T(4,128)S(1)} %bitcast.23, s32[8]{0:T(128)S(1)} %bitcast.30, f32[32,32,128]{2,1,0:T(8,128)S(1)} %bitcast.20, f32[32,32,128]{2,1,0:T(8,128)S(1)} %bitcast.19), custom_call_target="tpu_custom_call" | custom-call | tf_op jit(solution)/shard_map/sections_a/pallas_call | solution.py:182
  16.5 6.1 %collective-permute-done.3.refs_5_ = f32[32,32,128]{2,1,0:T(8,128)S(1)} collective-permute-done((f32[32,32,128]{2,1,0:T(8,128)S(1)}, f32[32,32,128]{2,1,0:T(8,128)S(1)}, u32[]{:S(2)}, u32[]{:S(2)}) %collective-permute-start.3) | collective-permute-done | bytes 524320 | tf_op jit(solution)/shard_map/ppermute | solution.py:30
  22.6 7.0 %collective-permute-start.6 = (f32[32,32,128]{2,1,0:T(8,128)S(1)}, f32[32,32,128]{2,1,0:T(8,128)S(1)}, u32[]{:S(2)}, u32[]{:S(2)}) collective-permute-start(f32[32,32,128]{2,1,0:T(8,128)S(1)} %bitcast.21), channel_id=1, source_target_pairs={{0,24},{1,25},{2,26},{3,27},{4,28},{5,29},{6,30},{7,31},{8,0},{9,1... | collective-permute-start | bytes 1572872 | tf_op jit(solution)/shard_map/ppermute | solution.py:30
  29.6 2.5 %collective-permute-done.1.refs_5_ = f32[32,32,128]{2,1,0:T(8,128)S(1)} collective-permute-done((f32[32,32,128]{2,1,0:T(8,128)S(1)}, f32[32,32,128]{2,1,0:T(8,128)S(1)}, u32[]{:S(2)}, u32[]{:S(2)}) %collective-permute-start.1) | collective-permute-done | bytes 524320 | tf_op jit(solution)/shard_map/ppermute | solution.py:30
  32.1 2.4 %collective-permute-done.refs_4_ = f32[32,32,128]{2,1,0:T(8,128)S(1)} collective-permute-done((f32[32,32,128]{2,1,0:T(8,128)S(1)}, f32[32,32,128]{2,1,0:T(8,128)S(1)}, u32[]{:S(2)}, u32[]{:S(2)}) %collective-permute-start) | collective-permute-done | bytes 524320 | tf_op jit(solution)/shard_map/ppermute | solution.py:30
  34.6 0.6 collective-permute-start.5
  35.2 1.4 %collective-permute-start.4 = (f32[32,32,128]{2,1,0:T(8,128)S(1)}, f32[32,32,128]{2,1,0:T(8,128)S(1)}, u32[]{:S(2)}, u32[]{:S(2)}) collective-permute-start(f32[32,32,128]{2,1,0:T(8,128)S(1)} %collective-permute-done.3.refs_5_), channel_id=1, source_target_pairs={{0,192},{1,193},{2,194},{3,195},{4,196},{5,197},{6,198},{7,199},{8... | collective-permute-start | bytes 1572872 | tf_op jit(solution)/shard_map/ppermute | solution.py:30
  36.6 7.4 %collective-permute-done.6.refs_3_ = f32[32,32,128]{2,1,0:T(8,128)S(1)} collective-permute-done((f32[32,32,128]{2,1,0:T(8,128)S(1)}, f32[32,32,128]{2,1,0:T(8,128)S(1)}, u32[]{:S(2)}, u32[]{:S(2)}) %collective-permute-start.6) | collective-permute-done | bytes 524320 | tf_op jit(solution)/shard_map/ppermute | solution.py:30
  44.0 1.8 %collective-permute-start.7 = (f32[32,32,128]{2,1,0:T(8,128)S(1)}, f32[32,32,128]{2,1,0:T(8,128)S(1)}, u32[]{:S(2)}, u32[]{:S(2)}) collective-permute-start(f32[32,32,128]{2,1,0:T(8,128)S(1)} %collective-permute-done.6.refs_3_), channel_id=1, source_target_pairs={{0,24},{1,25},{2,26},{3,27},{4,28},{5,29},{6,30},{7,31},{8,0},{9,1... | collective-permute-start | bytes 1572872 | tf_op jit(solution)/shard_map/ppermute | solution.py:30
  45.8 1.2 %collective-permute-start.11 = (f32[32,32,128]{2,1,0:T(8,128)S(1)}, f32[32,32,128]{2,1,0:T(8,128)S(1)}, u32[]{:S(2)}, u32[]{:S(2)}) collective-permute-start(f32[32,32,128]{2,1,0:T(8,128)S(1)} %collective-permute-done.3.refs_5_), channel_id=1, source_target_pairs={{0,128},{1,129},{2,130},{3,131},{4,132},{5,133},{6,134},{7,135},{8... | collective-permute-start | bytes 1572872 | tf_op jit(solution)/shard_map/ppermute | solution.py:30
  47.0 3.2 %sections_b.1 = (f32[129,32,128]{2,1,0:T(8,128)S(1)}, bf16[32,128,128]{2,1,0:T(8,128)(2,1)S(1)}) custom-call(s32[3]{0:T(128)S(1)} %pad_add_fusion.refs_0_, s32[8,3,64]{2,1,0:T(4,128)S(1)} %bitcast.24, s32[8]{0:T(128)S(1)} %bitcast.31, f32[32,32,128]{2,1,0:T(8,128)S(1)} %collective-permute-done.6.refs_3_, f32[32,32,128]{2,1,0:T(8,128)S(1)} %collective-permute-done.refs_4_, ...), custom_call_target="tpu_custom_call" | custom-call | tf_op jit(solution)/shard_map/sections_b/pallas_call | solution.py:182
  50.2 0.3 collective-permute-start.9
  50.6 0.0 collective-permute-done.4.refs_6_
  50.6 6.0 %collective-permute-done.7.refs_4_ = f32[32,32,128]{2,1,0:T(8,128)S(1)} collective-permute-done((f32[32,32,128]{2,1,0:T(8,128)S(1)}, f32[32,32,128]{2,1,0:T(8,128)S(1)}, u32[]{:S(2)}, u32[]{:S(2)}) %collective-permute-start.7) | collective-permute-done | bytes 524320 | tf_op jit(solution)/shard_map/ppermute | solution.py:30
  56.6 0.0 collective-permute-start.10
  56.6 4.3 %collective-permute-start.8 = (f32[32,32,128]{2,1,0:T(8,128)S(1)}, f32[32,32,128]{2,1,0:T(8,128)S(1)}, u32[]{:S(2)}, u32[]{:S(2)}) collective-permute-start(f32[32,32,128]{2,1,0:T(8,128)S(1)} %collective-permute-done.7.refs_4_), channel_id=1, source_target_pairs={{0,24},{1,25},{2,26},{3,27},{4,28},{5,29},{6,30},{7,31},{8,0},{9,1... | collective-permute-start | bytes 1572872 | tf_op jit(solution)/shard_map/ppermute | solution.py:30
  60.9 4.5 %sections_c.1.refs_9_ = f32[129,32,128]{2,1,0:T(8,128)S(1)} custom-call(s32[3]{0:T(128)S(1)} %pad_add_fusion.refs_0_, s32[8,3,64]{2,1,0:T(4,128)S(1)} %bitcast.25, s32[8]{0:T(128)S(1)} %bitcast.32, f32[32,32,128]{2,1,0:T(8,128)S(1)} %collective-permute-done.12.refs_3_, f32[32,32,128]{2,1,0:T(8,128)S(1)} %collective-permute-done.7.refs_4_, ...), custom_call_target="tpu_custom_call" | custom-call | tf_op jit(solution)/shard_map/sections_c/pallas_call | solution.py:182
  65.4 5.1 %sections_d.1 = (f32[129,32,128]{2,1,0:T(8,128)S(1)}, bf16[32,128,128]{2,1,0:T(8,128)(2,1)S(1)}) custom-call(s32[3]{0:T(128)S(1)} %pad_add_fusion.refs_0_, s32[8,3,64]{2,1,0:T(4,128)S(1)} %bitcast.26, s32[8]{0:T(128)S(1)} %bitcast.33, f32[32,32,128]{2,1,0:T(8,128)S(1)} %collective-permute-done.9.refs_3_, f32[32,32,128]{2,1,0:T(8,128)S(1)} %collective-permute-done.10.refs_4_, ...), custom_call_target="tpu_custom_call" | custom-call | tf_op jit(solution)/shard_map/sections_d/pallas_call | solution.py:182
  70.5 2.2 %collective-permute-done.8.refs_3_ = f32[32,32,128]{2,1,0:T(8,128)S(1)} collective-permute-done((f32[32,32,128]{2,1,0:T(8,128)S(1)}, f32[32,32,128]{2,1,0:T(8,128)S(1)}, u32[]{:S(2)}, u32[]{:S(2)}) %collective-permute-start.8) | collective-permute-done | bytes 524320 | tf_op jit(solution)/shard_map/ppermute | solution.py:30
  72.7 2.2 %sections_e.1.refs_5_ = f32[129,32,128]{2,1,0:T(8,128)S(1)} custom-call(s32[3]{0:T(128)S(1)} %pad_add_fusion.refs_0_, s32[8,3,64]{2,1,0:T(4,128)S(1)} %bitcast.27, s32[8]{0:T(128)S(1)} %bitcast.34, f32[32,32,128]{2,1,0:T(8,128)S(1)} %collective-permute-done.8.refs_3_, bf16[32,128,128]{2,1,0:T(8,128)(2,1)S(1)} %get-tuple-element.57.refs_4_, ...), custom_call_target="tpu_custom_call" | custom-call | tf_op jit(solution)/shard_map/sections_e/pallas_call | solution.py:182
  74.9 2.1 %sections_f1.1 = (f32[32,16,128]{2,1,0:T(8,128)S(1)}, f32[16,16,128]{2,1,0:T(8,128)S(1)}, f32[32,16,128]{2,1,0:T(8,128)S(1)}, f32[32,16,128]{2,1,0:T(8,128)S(1)}, f32[16,16,128]{2,1,0:T(8,128)S(1)}) custom-call(s32[3]{0:T(128)S(1)} %pad_add_fusion.refs_0_, s32[8,3,64]{2,1,0:T(4,128)S(1)} %bitcast.28, s32[8]{0:T(128)S(1)} %bitcast.35, ...), custom_call_target="tpu_custom_call" | custom-call | tf_op jit(solution)/shard_map/sections_f1/pallas_call | solution.py:182
  77.1 0.6 collective-permute-start.18
  77.7 1.5 %collective-permute-start.19 = (f32[32,16,128]{2,1,0:T(8,128)S(1)}, f32[32,16,128]{2,1,0:T(8,128)S(1)}, u32[]{:S(2)}, u32[]{:S(2)}) collective-permute-start(f32[32,16,128]{2,1,0:T(8,128)S(1)} %get-tuple-element.70), channel_id=1, source_target_pairs={{0,3},{1,0},{2,1},{3,2},{4,7},{5,4},{6,5},{7,6},{8,11},{9,8},{10,9... | collective-permute-start | bytes 786440 | tf_op jit(solution)/shard_map/ppermute | solution.py:30
  79.2 2.1 %sections_f0.1 = (f32[32,16,128]{2,1,0:T(8,128)S(1)}, f32[16,16,128]{2,1,0:T(8,128)S(1)}, f32[32,16,128]{2,1,0:T(8,128)S(1)}, f32[32,16,128]{2,1,0:T(8,128)S(1)}, f32[16,16,128]{2,1,0:T(8,128)S(1)}) custom-call(s32[3]{0:T(128)S(1)} %pad_add_fusion.refs_0_, s32[8,3,64]{2,1,0:T(4,128)S(1)} %bitcast.29, s32[8]{0:T(128)S(1)} %bitcast.36, ...), custom_call_target="tpu_custom_call" | custom-call | tf_op jit(solution)/shard_map/sections_f0/pallas_call | solution.py:182
  81.3 1.8 %collective-permute-start.14 = (f32[32,16,128]{2,1,0:T(8,128)S(1)}, f32[32,16,128]{2,1,0:T(8,128)S(1)}, u32[]{:S(2)}, u32[]{:S(2)}) collective-permute-start(f32[32,16,128]{2,1,0:T(8,128)S(1)} %get-tuple-element.60), channel_id=1, source_target_pairs={{0,1},{1,2},{2,3},{3,0},{4,5},{5,6},{6,7},{7,4},{8,9},{9,10},{10,1... | collective-permute-start | bytes 786440 | tf_op jit(solution)/shard_map/ppermute | solution.py:30
  83.2 0.3 collective-permute-start.15
  83.4 2.8 %collective-permute-done.18 = f32[32,16,128]{2,1,0:T(8,128)S(1)} collective-permute-done((f32[32,16,128]{2,1,0:T(8,128)S(1)}, f32[32,16,128]{2,1,0:T(8,128)S(1)}, u32[]{:S(2)}, u32[]{:S(2)}) %collective-permute-start.18) | collective-permute-done | bytes 262176 | tf_op jit(solution)/shard_map/ppermute | solution.py:30
  86.3 1.7 %collective-permute-done.19 = f32[32,16,128]{2,1,0:T(8,128)S(1)} collective-permute-done((f32[32,16,128]{2,1,0:T(8,128)S(1)}, f32[32,16,128]{2,1,0:T(8,128)S(1)}, u32[]{:S(2)}, u32[]{:S(2)}) %collective-permute-start.19) | collective-permute-done | bytes 262176 | tf_op jit(solution)/shard_map/ppermute | solution.py:30
  88.0 0.4 collective-permute-start.20
  88.5 1.7 %collective-permute-start.21 = (f32[16,16,128]{2,1,0:T(8,128)S(1)}, f32[16,16,128]{2,1,0:T(8,128)S(1)}, u32[]{:S(2)}, u32[]{:S(2)}) collective-permute-start(f32[16,16,128]{2,1,0:T(8,128)S(1)} %slice_add_fusion), channel_id=1, source_target_pairs={{0,3},{1,0},{2,1},{3,2},{4,7},{5,4},{6,5},{7,6},{8,11},{9,8},{10,9... | collective-permute-start | bytes 393224 | tf_op jit(solution)/shard_map/ppermute | solution.py:30
  90.2 1.7 %collective-permute-done.14 = f32[32,16,128]{2,1,0:T(8,128)S(1)} collective-permute-done((f32[32,16,128]{2,1,0:T(8,128)S(1)}, f32[32,16,128]{2,1,0:T(8,128)S(1)}, u32[]{:S(2)}, u32[]{:S(2)}) %collective-permute-start.14) | collective-permute-done | bytes 262176 | tf_op jit(solution)/shard_map/ppermute | solution.py:30
  91.9 1.7 %collective-permute-done.15 = f32[32,16,128]{2,1,0:T(8,128)S(1)} collective-permute-done((f32[32,16,128]{2,1,0:T(8,128)S(1)}, f32[32,16,128]{2,1,0:T(8,128)S(1)}, u32[]{:S(2)}, u32[]{:S(2)}) %collective-permute-start.15) | collective-permute-done | bytes 262176 | tf_op jit(solution)/shard_map/ppermute | solution.py:30
  93.6 0.4 collective-permute-start.16
  94.1 0.0 copy-start.1
  94.1 1.7 %collective-permute-start.17 = (f32[16,16,128]{2,1,0:T(8,128)S(1)}, f32[16,16,128]{2,1,0:T(8,128)S(1)}, u32[]{:S(2)}, u32[]{:S(2)}) collective-permute-start(f32[16,16,128]{2,1,0:T(8,128)S(1)} %slice_add_fusion.2), channel_id=1, source_target_pairs={{0,3},{1,0},{2,1},{3,2},{4,7},{5,4},{6,5},{7,6},{8,11},{9,8},{10,9... | collective-permute-start | bytes 393224 | tf_op jit(solution)/shard_map/ppermute | solution.py:30
  95.8 2.8 %collective-permute-done.16 = f32[16,16,128]{2,1,0:T(8,128)S(1)} collective-permute-done((f32[16,16,128]{2,1,0:T(8,128)S(1)}, f32[16,16,128]{2,1,0:T(8,128)S(1)}, u32[]{:S(2)}, u32[]{:S(2)}) %collective-permute-start.16) | collective-permute-done | bytes 131104 | tf_op jit(solution)/shard_map/ppermute | solution.py:30
  98.7 1.7 %collective-permute-done.17 = f32[16,16,128]{2,1,0:T(8,128)S(1)} collective-permute-done((f32[16,16,128]{2,1,0:T(8,128)S(1)}, f32[16,16,128]{2,1,0:T(8,128)S(1)}, u32[]{:S(2)}, u32[]{:S(2)}) %collective-permute-start.17) | collective-permute-done | bytes 131104 | tf_op jit(solution)/shard_map/ppermute | solution.py:30
  100.3 0.1 add_add_fusion.1
  100.5 0.1 maximum_multiply_fusion
  100.5 0.1 mul.27
  100.6 0.8 multiply_subtract_fusion
  (19 shorter events, 0.1 us)
Async XLA Ops:
  0.0 13.8 %copy-start = (s32[1,1,1,8]{3,2,1,0:T(1,128)S(1)}, s32[1,1,1,8]{3,2,1,0:T(1,128)}, u32[]{:S(2)}) copy-start(s32[1,1,1,8]{3,2,1,0:T(1,128)} %param.9) | copy-start | bytes 100
  1.2 21.5 %collective-permute-start.3 = (f32[32,32,128]{2,1,0:T(8,128)S(1)}, f32[32,32,128]{2,1,0:T(8,128)S(1)}, u32[]{:S(2)}, u32[]{:S(2)}) collective-permute-start(f32[32,32,128]{2,1,0:T(8,128)S(1)} %bitcast.15), channel_id=1, source_target_pairs={{0,32},{1,33},{2,34},{3,35},{4,36},{5,37},{6,38},{7,39},{8,40},{9,... | collective-permute-start | bytes 1572872 | tf_op jit(solution)/shard_map/ppermute | solution.py:30
  8.4 21.2 %collective-permute-start.2 = (f32[32,32,128]{2,1,0:T(8,128)S(1)}, f32[32,32,128]{2,1,0:T(8,128)S(1)}, u32[]{:S(2)}, u32[]{:S(2)}) collective-permute-start(f32[32,32,128]{2,1,0:T(8,128)S(1)} %bitcast.16), channel_id=1, source_target_pairs={{0,128},{1,129},{2,130},{3,131},{4,132},{5,133},{6,134},{7,135},{8... | collective-permute-start | bytes 1572872 | tf_op jit(solution)/shard_map/ppermute | solution.py:30
  9.7 22.5 %collective-permute-start.1 = (f32[32,32,128]{2,1,0:T(8,128)S(1)}, f32[32,32,128]{2,1,0:T(8,128)S(1)}, u32[]{:S(2)}, u32[]{:S(2)}) collective-permute-start(f32[32,32,128]{2,1,0:T(8,128)S(1)} %bitcast.17), channel_id=1, source_target_pairs={{0,64},{1,65},{2,66},{3,67},{4,68},{5,69},{6,70},{7,71},{8,72},{9,... | collective-permute-start | bytes 1572872 | tf_op jit(solution)/shard_map/ppermute | solution.py:30
  11.8 22.7 %collective-permute-start = (f32[32,32,128]{2,1,0:T(8,128)S(1)}, f32[32,32,128]{2,1,0:T(8,128)S(1)}, u32[]{:S(2)}, u32[]{:S(2)}) collective-permute-start(f32[32,32,128]{2,1,0:T(8,128)S(1)} %bitcast.18), channel_id=1, source_target_pairs={{0,192},{1,193},{2,194},{3,195},{4,196},{5,197},{6,198},{7,199},{8... | collective-permute-start | bytes 1572872 | tf_op jit(solution)/shard_map/ppermute | solution.py:30
  22.6 21.4 %collective-permute-start.6 = (f32[32,32,128]{2,1,0:T(8,128)S(1)}, f32[32,32,128]{2,1,0:T(8,128)S(1)}, u32[]{:S(2)}, u32[]{:S(2)}) collective-permute-start(f32[32,32,128]{2,1,0:T(8,128)S(1)} %bitcast.21), channel_id=1, source_target_pairs={{0,24},{1,25},{2,26},{3,27},{4,28},{5,29},{6,30},{7,31},{8,0},{9,1... | collective-permute-start | bytes 1572872 | tf_op jit(solution)/shard_map/ppermute | solution.py:30
  34.6 15.7 %collective-permute-start.5 = (f32[32,32,128]{2,1,0:T(8,128)S(1)}, f32[32,32,128]{2,1,0:T(8,128)S(1)}, u32[]{:S(2)}, u32[]{:S(2)}) collective-permute-start(f32[32,32,128]{2,1,0:T(8,128)S(1)} %collective-permute-done.3.refs_5_), channel_id=1, source_target_pairs={{0,64},{1,65},{2,66},{3,67},{4,68},{5,69},{6,70},{7,71},{8,72},{9,... | collective-permute-start | bytes 1572872 | tf_op jit(solution)/shard_map/ppermute | solution.py:30
  35.2 15.4 %collective-permute-start.4 = (f32[32,32,128]{2,1,0:T(8,128)S(1)}, f32[32,32,128]{2,1,0:T(8,128)S(1)}, u32[]{:S(2)}, u32[]{:S(2)}) collective-permute-start(f32[32,32,128]{2,1,0:T(8,128)S(1)} %collective-permute-done.3.refs_5_), channel_id=1, source_target_pairs={{0,192},{1,193},{2,194},{3,195},{4,196},{5,197},{6,198},{7,199},{8... | collective-permute-start | bytes 1572872 | tf_op jit(solution)/shard_map/ppermute | solution.py:30
  44.0 12.6 %collective-permute-start.7 = (f32[32,32,128]{2,1,0:T(8,128)S(1)}, f32[32,32,128]{2,1,0:T(8,128)S(1)}, u32[]{:S(2)}, u32[]{:S(2)}) collective-permute-start(f32[32,32,128]{2,1,0:T(8,128)S(1)} %collective-permute-done.6.refs_3_), channel_id=1, source_target_pairs={{0,24},{1,25},{2,26},{3,27},{4,28},{5,29},{6,30},{7,31},{8,0},{9,1... | collective-permute-start | bytes 1572872 | tf_op jit(solution)/shard_map/ppermute | solution.py:30
  45.8 15.1 %collective-permute-start.12 = (f32[32,32,128]{2,1,0:T(8,128)S(1)}, f32[32,32,128]{2,1,0:T(8,128)S(1)}, u32[]{:S(2)}, u32[]{:S(2)}) collective-permute-start(f32[32,32,128]{2,1,0:T(8,128)S(1)} %bitcast.22), channel_id=1, source_target_pairs={{0,4},{1,5},{2,6},{3,7},{4,0},{5,1},{6,2},{7,3},{8,12},{9,13},{10,... | collective-permute-start | bytes 1572872 | tf_op jit(solution)/shard_map/ppermute | solution.py:30
  45.8 19.6 %collective-permute-start.11 = (f32[32,32,128]{2,1,0:T(8,128)S(1)}, f32[32,32,128]{2,1,0:T(8,128)S(1)}, u32[]{:S(2)}, u32[]{:S(2)}) collective-permute-start(f32[32,32,128]{2,1,0:T(8,128)S(1)} %collective-permute-done.3.refs_5_), channel_id=1, source_target_pairs={{0,128},{1,129},{2,130},{3,131},{4,132},{5,133},{6,134},{7,135},{8... | collective-permute-start | bytes 1572872 | tf_op jit(solution)/shard_map/ppermute | solution.py:30
  50.2 15.2 %collective-permute-start.9 = (f32[32,32,128]{2,1,0:T(8,128)S(1)}, f32[32,32,128]{2,1,0:T(8,128)S(1)}, u32[]{:S(2)}, u32[]{:S(2)}) collective-permute-start(f32[32,32,128]{2,1,0:T(8,128)S(1)} %collective-permute-done.6.refs_3_), channel_id=1, source_target_pairs={{0,4},{1,5},{2,6},{3,7},{4,0},{5,1},{6,2},{7,3},{8,12},{9,13},{10,... | collective-permute-start | bytes 1572872 | tf_op jit(solution)/shard_map/ppermute | solution.py:30
  56.6 8.8 %collective-permute-start.10 = (f32[32,32,128]{2,1,0:T(8,128)S(1)}, f32[32,32,128]{2,1,0:T(8,128)S(1)}, u32[]{:S(2)}, u32[]{:S(2)}) collective-permute-start(f32[32,32,128]{2,1,0:T(8,128)S(1)} %collective-permute-done.7.refs_4_), channel_id=1, source_target_pairs={{0,4},{1,5},{2,6},{3,7},{4,0},{5,1},{6,2},{7,3},{8,12},{9,13},{10,... | collective-permute-start | bytes 1572872 | tf_op jit(solution)/shard_map/ppermute | solution.py:30
  56.6 16.1 %collective-permute-start.8 = (f32[32,32,128]{2,1,0:T(8,128)S(1)}, f32[32,32,128]{2,1,0:T(8,128)S(1)}, u32[]{:S(2)}, u32[]{:S(2)}) collective-permute-start(f32[32,32,128]{2,1,0:T(8,128)S(1)} %collective-permute-done.7.refs_4_), channel_id=1, source_target_pairs={{0,24},{1,25},{2,26},{3,27},{4,28},{5,29},{6,30},{7,31},{8,0},{9,1... | collective-permute-start | bytes 1572872 | tf_op jit(solution)/shard_map/ppermute | solution.py:30
  72.7 2.2 %collective-permute-start.13 = (f32[32,32,128]{2,1,0:T(8,128)S(1)}, f32[32,32,128]{2,1,0:T(8,128)S(1)}, u32[]{:S(2)}, u32[]{:S(2)}) collective-permute-start(f32[32,32,128]{2,1,0:T(8,128)S(1)} %collective-permute-done.8.refs_3_), channel_id=1, source_target_pairs={{0,4},{1,5},{2,6},{3,7},{4,0},{5,1},{6,2},{7,3},{8,12},{9,13},{10,... | collective-permute-start | bytes 1572872 | tf_op jit(solution)/shard_map/ppermute | solution.py:30
  77.1 9.2 %collective-permute-start.18 = (f32[32,16,128]{2,1,0:T(8,128)S(1)}, f32[32,16,128]{2,1,0:T(8,128)S(1)}, u32[]{:S(2)}, u32[]{:S(2)}) collective-permute-start(f32[32,16,128]{2,1,0:T(8,128)S(1)} %get-tuple-element.69), channel_id=1, source_target_pairs={{0,1},{1,2},{2,3},{3,0},{4,5},{5,6},{6,7},{7,4},{8,9},{9,10},{10,1... | collective-permute-start | bytes 786440 | tf_op jit(solution)/shard_map/ppermute | solution.py:30
  77.7 10.3 %collective-permute-start.19 = (f32[32,16,128]{2,1,0:T(8,128)S(1)}, f32[32,16,128]{2,1,0:T(8,128)S(1)}, u32[]{:S(2)}, u32[]{:S(2)}) collective-permute-start(f32[32,16,128]{2,1,0:T(8,128)S(1)} %get-tuple-element.70), channel_id=1, source_target_pairs={{0,3},{1,0},{2,1},{3,2},{4,7},{5,4},{6,5},{7,6},{8,11},{9,8},{10,9... | collective-permute-start | bytes 786440 | tf_op jit(solution)/shard_map/ppermute | solution.py:30
  81.3 10.5 %collective-permute-start.14 = (f32[32,16,128]{2,1,0:T(8,128)S(1)}, f32[32,16,128]{2,1,0:T(8,128)S(1)}, u32[]{:S(2)}, u32[]{:S(2)}) collective-permute-start(f32[32,16,128]{2,1,0:T(8,128)S(1)} %get-tuple-element.60), channel_id=1, source_target_pairs={{0,1},{1,2},{2,3},{3,0},{4,5},{5,6},{6,7},{7,4},{8,9},{9,10},{10,1... | collective-permute-start | bytes 786440 | tf_op jit(solution)/shard_map/ppermute | solution.py:30
  83.2 10.4 %collective-permute-start.15 = (f32[32,16,128]{2,1,0:T(8,128)S(1)}, f32[32,16,128]{2,1,0:T(8,128)S(1)}, u32[]{:S(2)}, u32[]{:S(2)}) collective-permute-start(f32[32,16,128]{2,1,0:T(8,128)S(1)} %get-tuple-element.61), channel_id=1, source_target_pairs={{0,3},{1,0},{2,1},{3,2},{4,7},{5,4},{6,5},{7,6},{8,11},{9,8},{10,9... | collective-permute-start | bytes 786440 | tf_op jit(solution)/shard_map/ppermute | solution.py:30
  88.0 7.8 %collective-permute-start.20 = (f32[16,16,128]{2,1,0:T(8,128)S(1)}, f32[16,16,128]{2,1,0:T(8,128)S(1)}, u32[]{:S(2)}, u32[]{:S(2)}) collective-permute-start(f32[16,16,128]{2,1,0:T(8,128)S(1)} %slice_add_fusion.1), channel_id=1, source_target_pairs={{0,1},{1,2},{2,3},{3,0},{4,5},{5,6},{6,7},{7,4},{8,9},{9,10},{10,1... | collective-permute-start | bytes 393224 | tf_op jit(solution)/shard_map/ppermute | solution.py:30
  88.5 7.4 %collective-permute-start.21 = (f32[16,16,128]{2,1,0:T(8,128)S(1)}, f32[16,16,128]{2,1,0:T(8,128)S(1)}, u32[]{:S(2)}, u32[]{:S(2)}) collective-permute-start(f32[16,16,128]{2,1,0:T(8,128)S(1)} %slice_add_fusion), channel_id=1, source_target_pairs={{0,3},{1,0},{2,1},{3,2},{4,7},{5,4},{6,5},{7,6},{8,11},{9,8},{10,9... | collective-permute-start | bytes 393224 | tf_op jit(solution)/shard_map/ppermute | solution.py:30
  93.6 5.0 %collective-permute-start.16 = (f32[16,16,128]{2,1,0:T(8,128)S(1)}, f32[16,16,128]{2,1,0:T(8,128)S(1)}, u32[]{:S(2)}, u32[]{:S(2)}) collective-permute-start(f32[16,16,128]{2,1,0:T(8,128)S(1)} %slice_add_fusion.3), channel_id=1, source_target_pairs={{0,1},{1,2},{2,3},{3,0},{4,5},{5,6},{6,7},{7,4},{8,9},{9,10},{10,1... | collective-permute-start | bytes 393224 | tf_op jit(solution)/shard_map/ppermute | solution.py:30
  94.1 6.6 %copy-start.1 = (f32[1,1,32,4096]{3,2,1,0:T(8,128)S(1)}, f32[1,1,32,4096]{3,2,1,0:T(8,128)}, u32[]{:S(2)}) copy-start(f32[1,1,32,4096]{3,2,1,0:T(8,128)} %param.7) | copy-start | bytes 1572868
  94.1 6.3 %collective-permute-start.17 = (f32[16,16,128]{2,1,0:T(8,128)S(1)}, f32[16,16,128]{2,1,0:T(8,128)S(1)}, u32[]{:S(2)}, u32[]{:S(2)}) collective-permute-start(f32[16,16,128]{2,1,0:T(8,128)S(1)} %slice_add_fusion.2), channel_id=1, source_target_pairs={{0,3},{1,0},{2,1},{3,2},{4,7},{5,4},{6,5},{7,6},{8,11},{9,8},{10,9... | collective-permute-start | bytes 393224 | tf_op jit(solution)/shard_map/ppermute | solution.py:30
